TPU v7x, 32 devices: a whole 2x2x4 slice. The times are simulated.
32 devices in a mesh: dp: 8 (over z, x), mp: 4 (over y, core).
Axes of the slice: x: 2, y: 2, z: 4, core: 2. Of those that a mesh axis runs over, the one named last changes fastest.
Arguments:
- tokens: bfloat16 [16, 680, 1024], P('dp'), may hold values from -6 to 6
- cotangent: bfloat16 [16, 680, 1024], P('dp'), may hold values from -6 to 6
- stop_scales: int32 [16], P('dp'), may hold values from 6 to 10, as said below
- labels: int32 [16], P('dp'), may hold values from 0 to 1000
- class_table: bfloat16 [1001, 1024], P(None, 'mp'), may hold values from -6 to 6
- ada_weight: bfloat16 [1024, 6144], P('mp'), may hold values from -0.09375 to 0.09375
- ada_bias: float32 [6144], replicated, may hold values from 0.5 to 1.5
- qkv_weight: bfloat16 [1024, 3, 1024], P(None, None, 'mp'), may hold values from -0.1875 to 0.1875
- qv_bias: float32 [2, 1024], P(None, 'mp'), may hold values from -5 to 5
- log_scale: float32 [16], P('mp'), may hold values from 2 to 3.2
- proj_weight: bfloat16 [1024, 1024], P('mp'), may hold values from -0.75 to 0.75
- proj_bias: float32 [1024], replicated, may hold values from -3 to 3
- fc1_weight: bfloat16 [1024, 4096], P(None, 'mp'), may hold values from -0.1875 to 0.1875
- fc1_bias: float32 [4096], P('mp'), may hold values from -3 to 3
- fc2_weight: bfloat16 [4096, 1024], P('mp'), may hold values from -0.09375 to 0.09375
- fc2_bias: float32 [1024], replicated, may hold values from -3 to 3
Outputs:
- block_out: bfloat16 [16, 680, 1024], P('dp')
- token_grad: bfloat16 [16, 680, 1024], P('dp')
- table_grad: float32 [1001, 1024], P(None, 'mp')
- ada_weight_grad: float32 [1024, 6144], P('mp')
- ada_bias_grad: float32 [6144], replicated
- qkv_weight_grad: float32 [1024, 3, 1024], P(None, None, 'mp')
- qv_bias_grad: float32 [2, 1024], P(None, 'mp')
- log_scale_grad: float32 [16], P('mp')
- proj_weight_grad: float32 [1024, 1024], P('mp')
- proj_bias_grad: float32 [1024], replicated
- fc1_weight_grad: float32 [1024, 4096], P(None, 'mp')
- fc1_bias_grad: float32 [4096], P('mp')
- fc2_weight_grad: float32 [4096, 1024], P('mp')
- fc2_bias_grad: float32 [1024], replicated
Inputs may be any that keep to these rules, and one draw needn't show every extreme that they name: `stop_scales`: an item with stop scale s has its first 1, 5, 14, 30, 55, 91, 155, 255, 424 or 680 slots live for s = 1 to 10; in every draw some item stops at 10 and some at 6.
All inputs are finite; a program needn't handle non-finite values.
Results may differ from a plain program's by a relative error of at most 0.028.
Values sent between devices are 32-bit elements; how exact they have to be, the bound alone decides.
A program may use at most 192 MiB of HBM per device.

v0:
```python
import jax
import jax.numpy as jnp
import numpy as np
from jax import lax
from jax.sharding import PartitionSpec as P

SIDE_LIST = (1, 2, 3, 4, 5, 6, 8, 10, 13, 16)
EPSILON = 1e-06


def scale_table(stop_scales, slot_count):
    scale_ends = np.cumsum(np.array([side_length * side_length for side_length in SIDE_LIST]))
    positions = jnp.arange(slot_count, dtype=jnp.int32)
    bounds = jnp.asarray(scale_ends[:-1], dtype=jnp.int32)
    levels = jnp.sum((positions[:, None] >= bounds[None, :]).astype(jnp.int32), axis=1)
    counters = jnp.arange(1, len(SIDE_LIST) + 1, dtype=jnp.int32)
    ends_array = jnp.asarray(scale_ends, dtype=jnp.int32)
    lengths = jnp.sum(
        jnp.where(stop_scales[:, None] == counters[None, :], ends_array[None, :], 0), axis=1
    )
    return (positions, levels, lengths)


def modulate(row_block, scale_row, shift_row):
    center = row_block - jnp.mean(row_block, axis=-1, keepdims=True)
    spread = jnp.mean(center * center, axis=-1, keepdims=True)
    return center * lax.rsqrt(spread + EPSILON) * (1.0 + scale_row) + shift_row


def unit_heads(query_rows, key_rows, head_scale):
    query_unit = (
        query_rows
        * lax.rsqrt(jnp.sum(query_rows * query_rows, axis=-1, keepdims=True) + EPSILON)
        * jnp.exp(head_scale)[:, None]
    )
    key_unit = key_rows * lax.rsqrt(jnp.sum(key_rows * key_rows, axis=-1, keepdims=True) + EPSILON)
    return (query_unit, key_unit)


def gelu_tanh(values):
    return jax.nn.gelu(values, approximate=True)


def shards(
    tokens,
    cotangent,
    stop_scales,
    labels,
    class_table,
    ada_weight,
    ada_bias,
    qkv_weight,
    qv_bias,
    log_scale,
    proj_weight,
    proj_bias,
    fc1_weight,
    fc1_bias,
    fc2_weight,
    fc2_bias,
):
    item_count, slot_count, model_width = tokens.shape
    local_heads = log_scale.shape[0]
    local_width = qkv_weight.shape[2]
    head_size = local_width // local_heads
    row_count = item_count * slot_count
    classes = class_table.shape[0]
    positions, levels, lengths = scale_table(stop_scales, slot_count)
    onehot = (labels[:, None] == jnp.arange(classes, dtype=jnp.int32)[None, :]).astype(jnp.bfloat16)
    class_local = jnp.dot(onehot, class_table, preferred_element_type=jnp.float32)
    lifted_low = jax.nn.silu(class_local).astype(jnp.bfloat16)
    modulation = (
        lax.psum(jnp.dot(lifted_low, ada_weight, preferred_element_type=jnp.float32), "mp")
        + ada_bias
    )
    pieces = modulation.reshape(item_count, 6, 1, model_width)
    gamma_one = pieces[:, 0]
    gamma_two = pieces[:, 1]
    scale_one = pieces[:, 2]
    scale_two = pieces[:, 3]
    shift_one = pieces[:, 4]
    shift_two = pieces[:, 5]
    inputs = tokens.astype(jnp.float32)
    first_low = (
        modulate(inputs, scale_one, shift_one).astype(jnp.bfloat16).reshape(row_count, model_width)
    )
    bias_rows = jnp.stack([qv_bias[0], jnp.zeros_like(qv_bias[0]), qv_bias[1]])
    triple = (
        jnp.einsum("rd,dcf->rcf", first_low, qkv_weight, preferred_element_type=jnp.float32)
        + bias_rows
    )
    triple = triple.reshape(item_count, slot_count, 3, local_heads, head_size)
    query_rows = triple[:, :, 0]
    key_rows = triple[:, :, 1]
    value_low = triple[:, :, 2].astype(jnp.bfloat16)
    query_unit, key_unit = unit_heads(query_rows, key_rows, log_scale)
    query_low = query_unit.astype(jnp.bfloat16)
    key_low = key_unit.astype(jnp.bfloat16)

    def attend(packed):
        query_item, key_item, value_item, length = packed
        allowed = (levels[None, :] <= levels[:, None]) & (positions[None, :] < length)
        scores = jnp.einsum(
            "qhe,khe->hqk", query_item, key_item, preferred_element_type=jnp.float32
        )
        masked = jnp.where(allowed[None], scores, -1e30)
        row_peak = jnp.max(masked, axis=-1, keepdims=True)
        exp_terms = jnp.exp(masked - row_peak)
        row_total = jnp.sum(exp_terms, axis=-1, keepdims=True)
        probabilities = (exp_terms / row_total).astype(jnp.bfloat16)
        mixed_rows = jnp.einsum(
            "hqk,khe->qhe", probabilities, value_item, preferred_element_type=jnp.float32
        )
        return (mixed_rows.astype(jnp.bfloat16), row_peak[..., 0] + jnp.log(row_total[..., 0]))

    mixed_low, log_totals = lax.map(attend, (query_low, key_low, value_low, lengths))
    mixed_flat = mixed_low.reshape(row_count, local_width)
    attended = (
        lax.psum(
            jnp.dot(mixed_flat, proj_weight, preferred_element_type=jnp.float32), "mp"
        ).reshape(item_count, slot_count, model_width)
        + proj_bias
    )
    middle = inputs + gamma_one * attended
    second_low = (
        modulate(middle, scale_two, shift_two).astype(jnp.bfloat16).reshape(row_count, model_width)
    )
    upper = jnp.dot(second_low, fc1_weight, preferred_element_type=jnp.float32) + fc1_bias
    hidden_low = gelu_tanh(upper).astype(jnp.bfloat16)
    branch = (
        lax.psum(jnp.dot(hidden_low, fc2_weight, preferred_element_type=jnp.float32), "mp").reshape(
            item_count, slot_count, model_width
        )
        + fc2_bias
    )
    block_out = (middle + gamma_two * branch).astype(jnp.bfloat16)
    upstream = cotangent.astype(jnp.float32)
    grad_gamma_two = jnp.sum(upstream * branch, axis=1)
    branch_grad = (upstream * gamma_two).astype(jnp.bfloat16).reshape(row_count, model_width)
    fc2_bias_grad = jnp.sum(branch_grad.astype(jnp.float32), axis=0)
    fc2_weight_grad = jnp.einsum(
        "rf,rd->fd", hidden_low, branch_grad, preferred_element_type=jnp.float32
    )
    hidden_grad = jnp.einsum(
        "rd,fd->rf", branch_grad, fc2_weight, preferred_element_type=jnp.float32
    )
    upper_grad = jax.vjp(gelu_tanh, upper)[1](hidden_grad)[0].astype(jnp.bfloat16)
    fc1_bias_grad = jnp.sum(upper_grad.astype(jnp.float32), axis=0)
    fc1_weight_grad = jnp.einsum(
        "rd,rf->df", second_low, upper_grad, preferred_element_type=jnp.float32
    )
    second_grad = lax.psum(
        jnp.einsum("rf,df->rd", upper_grad, fc1_weight, preferred_element_type=jnp.float32), "mp"
    ).reshape(item_count, slot_count, model_width)
    mlp_grads = (fc1_weight_grad, fc1_bias_grad, fc2_weight_grad, fc2_bias_grad)
    second_back = jax.vjp(modulate, middle, scale_two, shift_two)[1]
    middle_norm_grad, scale_two_grad, shift_two_grad = second_back(second_grad)
    middle_grad = upstream + middle_norm_grad
    grad_gamma_one = jnp.sum(middle_grad * attended, axis=1)
    attended_grad = (middle_grad * gamma_one).astype(jnp.bfloat16).reshape(row_count, model_width)
    proj_bias_grad = jnp.sum(attended_grad.astype(jnp.float32), axis=0)
    proj_weight_grad = jnp.einsum(
        "rf,rd->fd", mixed_flat, attended_grad, preferred_element_type=jnp.float32
    )
    mixed_grad = jnp.einsum(
        "rd,fd->rf", attended_grad, proj_weight, preferred_element_type=jnp.float32
    ).astype(jnp.bfloat16)
    mixed_grad = mixed_grad.reshape(item_count, slot_count, local_heads, head_size)

    def attend_back(packed):
        query_item, key_item, value_item, mixed_item_grad, log_total, length = packed
        allowed = (levels[None, :] <= levels[:, None]) & (positions[None, :] < length)
        scores = jnp.einsum(
            "qhe,khe->hqk", query_item, key_item, preferred_element_type=jnp.float32
        )
        probabilities = jnp.where(allowed[None], jnp.exp(scores - log_total[..., None]), 0.0)
        probs_low = probabilities.astype(jnp.bfloat16)
        value_grad = jnp.einsum(
            "hqk,qhe->khe", probs_low, mixed_item_grad, preferred_element_type=jnp.float32
        )
        probs_grad = jnp.einsum(
            "qhe,khe->hqk", mixed_item_grad, value_item, preferred_element_type=jnp.float32
        )
        inner_sum = jnp.sum(probs_grad * probabilities, axis=-1, keepdims=True)
        score_grad = (probabilities * (probs_grad - inner_sum)).astype(jnp.bfloat16)
        query_grad = jnp.einsum(
            "hqk,khe->qhe", score_grad, key_item, preferred_element_type=jnp.float32
        )
        key_grad = jnp.einsum(
            "hqk,qhe->khe", score_grad, query_item, preferred_element_type=jnp.float32
        )
        return (query_grad, key_grad, value_grad)

    query_unit_grad, key_unit_grad, value_grad = lax.map(
        attend_back, (query_low, key_low, value_low, mixed_grad, log_totals, lengths)
    )
    unit_back = jax.vjp(unit_heads, query_rows, key_rows, log_scale)[1]
    query_pre_grad, key_pre_grad, log_scale_grad = unit_back((query_unit_grad, key_unit_grad))
    triple_grad = (
        jnp.stack([query_pre_grad, key_pre_grad, value_grad], axis=2)
        .astype(jnp.bfloat16)
        .reshape(row_count, 3, local_width)
    )
    qv_bias_grad = jnp.sum(triple_grad[:, 0::2].astype(jnp.float32), axis=0)
    qkv_weight_grad = jnp.einsum(
        "rd,rcf->dcf", first_low, triple_grad, preferred_element_type=jnp.float32
    )
    first_grad = lax.psum(
        jnp.einsum("rcf,dcf->rd", triple_grad, qkv_weight, preferred_element_type=jnp.float32), "mp"
    ).reshape(item_count, slot_count, model_width)
    first_back = jax.vjp(modulate, inputs, scale_one, shift_one)[1]
    input_norm_grad, scale_one_grad, shift_one_grad = first_back(first_grad)
    token_grad = (middle_grad + input_norm_grad).astype(jnp.bfloat16)
    modulation_grad = jnp.stack(
        [
            grad_gamma_one,
            grad_gamma_two,
            scale_one_grad[:, 0],
            scale_two_grad[:, 0],
            shift_one_grad[:, 0],
            shift_two_grad[:, 0],
        ],
        axis=1,
    )
    modulation_grad = modulation_grad.reshape(item_count, 6 * model_width).astype(jnp.bfloat16)
    ada_bias_grad = jnp.sum(modulation_grad.astype(jnp.float32), axis=0)
    ada_weight_grad = jnp.einsum(
        "id,ik->dk", lifted_low, modulation_grad, preferred_element_type=jnp.float32
    )
    lifted_grad = jnp.einsum(
        "ik,dk->id", modulation_grad, ada_weight, preferred_element_type=jnp.float32
    )
    class_grad = jax.vjp(jax.nn.silu, class_local)[1](lifted_grad)[0]
    every_class, every_label = (
        lax.all_gather(class_grad, "dp", axis=0, tiled=True),
        lax.all_gather(labels.astype(jnp.float32), "dp", axis=0, tiled=True),
    )
    class_hot = (every_label[:, None] == jnp.arange(classes, dtype=jnp.float32)[None, :]).astype(
        jnp.float32
    )
    table_grad = jnp.einsum("ic,id->cd", class_hot, every_class, precision=lax.Precision.HIGHEST)
    every_sum = lax.psum(
        (
            ada_weight_grad,
            ada_bias_grad,
            qkv_weight_grad,
            qv_bias_grad,
            log_scale_grad,
            proj_weight_grad,
            proj_bias_grad,
            mlp_grads[0],
            mlp_grads[1],
            mlp_grads[2],
            mlp_grads[3],
        ),
        "dp",
    )
    return (
        block_out,
        token_grad,
        table_grad,
        every_sum[0],
        every_sum[1],
        every_sum[2],
        every_sum[3],
        every_sum[4],
        every_sum[5],
        every_sum[6],
        every_sum[7],
        every_sum[8],
        every_sum[9],
        every_sum[10],
    )


def solution(mesh):
    return jax.shard_map(
        shards,
        mesh=mesh,
        in_specs=(
            P("dp", None, None),
            P("dp", None, None),
            P("dp"),
            P("dp"),
            P(None, "mp"),
            P("mp", None),
            P(),
            P(None, None, "mp"),
            P(None, "mp"),
            P("mp"),
            P("mp", None),
            P(),
            P(None, "mp"),
            P("mp"),
            P("mp", None),
            P(),
        ),
        out_specs=(
            P("dp", None, None),
            P("dp", None, None),
            P(None, "mp"),
            P("mp", None),
            P(),
            P(None, None, "mp"),
            P(None, "mp"),
            P("mp"),
            P("mp", None),
            P(),
            P(None, "mp"),
            P("mp"),
            P("mp", None),
            P(),
        ),
        check_vma=False,
    )
```

profile of v0, /device:TPU:0, one launch (start us, length us, event | category | flops | bytes accessed | tf_op | source)
XLA Modules:
  0.0 1312.3 jit_solution(17432782557219697358)
XLA Ops:
  8.2 2.4 convert_reduce_fusion
  10.6 2.7 fusion.69
  14.4 13.2 %psum.112 = f32[2,6144]{1,0:T(2,128)S(1)} all-reduce(f32[2,6144]{1,0:T(2,128)S(1)} %fusion.90), channel_id=1, replica_groups=mesh['dp'=8,'mp'=4] {'mp'}, use_global_device_ids=true, to_apply=%region_0.0 | all-reduce | flops 12288 | bytes 98304 | tf_op jit(solution)/shard_map/psum | solution.py:73
  28.5 2.5 fusion.60
  32.6 4.4 convolution_add_fusion
  37.0 5.7 copy.91
  42.7 7.5 reshape.322
  50.2 2.7 multiply_reduce_fusion.8
  52.9 2.8 fusion.76
  56.0 2.1 copy.92
  58.1 2.6 multiply_convert_fusion.3
  62.9 19.0 %while.28 = (s32[]{:T(128)}, bf16[2,680,4,64]{1,3,2,0:T(8,128)(2,1)}, f32[2,4,680]{2,1,0:T(4,128)S(1)}, bf16[2,680,4,64]{1,3,2,0:T(8,128)(2,1)}, s32[680]{0:T(10...) while((s32[]{:T(128)}, ...), condition=%wide.region_10.11_spmd.clone, body=%wide.region_7.10_spmd.clone.sunk | while | flops 491240864 | bytes 35091196 | solution.py:116
  64.6 2.6 select_reduce_fusion.2
  68.7 2.6 fusion.150
  73.9 2.6 select_reduce_fusion.2
  78.1 2.6 fusion.150
  81.8 2.8 copy.95
  84.7 3.0 reshape.323
  87.7 4.6 fusion.102
  92.4 4.9 convert_reduce_fusion.1
  97.3 103.3 %all-reduce.9.cloned.1.call-done = f32[2,680,1024]{2,1,0:T(8,128)} async-done(((f32[2,680,1024]{2,1,0:T(8,128)}), f32[2,680,1024]{2,1,0:T(8,128)}) %all-reduce.9.cloned.1.call-update) | async-done | bytes 5570576 | tf_op jit(solution)/shard_map/psum | solution.py:119
  200.7 4.5 fusion.99
  208.9 3.1 fusion.103
  212.0 7.3 convert_reduce_fusion.2
  219.3 4.9 fusion.104
  224.3 9.4 fusion.92
  233.7 98.7 %all-reduce.11.cloned.1.call-done = f32[2,680,1024]{2,1,0:T(8,128)} async-done(((f32[2,680,1024]{2,1,0:T(8,128)}), f32[2,680,1024]{2,1,0:T(8,128)}) %all-reduce.11.cloned.1.call-update) | async-done | bytes 5570576 | tf_op jit(solution)/shard_map/psum | solution.py:152
  332.4 17.7 %multiply_reduce_fusion.1 = (bf16[2,1024]{1,0:T(2,128)(2,1)}, f32[2,680]{1,0:T(2,128)S(1)}, bf16[2,1024]{1,0:T(2,128)(2,1)}) fusion(f32[2,680,1024]{2,1,0:T(8,128)} %all-reduce.11.cloned.1.call-done, f32[2,680,1024]{2,1,0:T(8,128)} %copy-done.1, f32[2,680]{1,0:T(2,128)S(1)} %fusion.84, f32[2,680]{1,0:T(2,128)S(1)} %broadcast_multiply_fusion, ...), kind=kLoop, calls=%fused_computation.93 | loop fusion | flops 11135664 | bytes 11173824 | tf_op jit(solution)/shard_map/transpose(jvp())/reduce_sum | solution.py:27
  350.2 3.6 fusion.98
  353.9 2.2 convert_reduce_fusion.3
  359.6 3.2 reshape.345
  362.8 3.3 copy.99
  366.1 94.2 %while.29 = (s32[]{:T(128)}, f32[2,680,4,64]{1,0,3,2:T(2,128)}, f32[2,680,4,64]{1,0,3,2:T(2,128)}, bf16[2,680,4,64]{1,3,2,0:T(8,128)(2,1)}, bf16[2,680,4,64]{1,3...) while((s32[]{:T(128)}, f32[2,680,4,64]{1,0,3,2:T(2,128)}, ...), condition=%wide.region_20.21_spmd.clone, body=%wide.region_18.20_spmd.clone.sunk | while | flops 1206861952 | bytes 81969152 | solution.py:194
  367.7 2.4 fusion.159
  370.1 2.5 fusion.160
  372.5 2.7 multiply_reduce_fusion.11
  383.0 15.1 %dynamic_update_slice.35 = f32[2,680,4,64]{1,0,3,2:T(2,128)} dynamic-update-slice(f32[2,680,4,64]{1,0,3,2:T(2,128)} %get-tuple-element.507, f32[1,680,4,64]{1,0,3,2:T(1,128)} %copy.160, s32[]{:T(128)S(6)} %copy.181, s32[]{:T(128)} %constant.72.clone.1..sunk, s32[]{:T(128)} %constant.72.clone.1..sunk, s32[]{:T(128)} %constant.72.clone.1..sunk) | dynamic-update-slice | bytes 1392644 | tf_op jit(solution)/shard_map/while/body/jit(dynamic_update_index_in_dim)/dynamic_update_slice | solution.py:194
  398.1 15.1 %dynamic_update_slice.34 = f32[2,680,4,64]{1,0,3,2:T(2,128)} dynamic-update-slice(f32[2,680,4,64]{1,0,3,2:T(2,128)} %get-tuple-element.506, f32[1,680,4,64]{1,0,3,2:T(1,128)} %copy.159, s32[]{:T(128)S(6)} %copy.181, s32[]{:T(128)} %constant.72.clone.1..sunk, s32[]{:T(128)} %constant.72.clone.1..sunk, s32[]{:T(128)} %constant.72.clone.1..sunk) | dynamic-update-slice | bytes 1392644 | tf_op jit(solution)/shard_map/while/body/jit(dynamic_update_index_in_dim)/dynamic_update_slice | solution.py:194
  414.7 2.4 fusion.159
  417.2 2.5 fusion.160
  419.6 2.7 multiply_reduce_fusion.11
  430.1 15.1 %dynamic_update_slice.35 = f32[2,680,4,64]{1,0,3,2:T(2,128)} dynamic-update-slice(f32[2,680,4,64]{1,0,3,2:T(2,128)} %get-tuple-element.507, f32[1,680,4,64]{1,0,3,2:T(1,128)} %copy.160, s32[]{:T(128)S(6)} %copy.181, s32[]{:T(128)} %constant.72.clone.1..sunk, s32[]{:T(128)} %constant.72.clone.1..sunk, s32[]{:T(128)} %constant.72.clone.1..sunk) | dynamic-update-slice | bytes 1392644 | tf_op jit(solution)/shard_map/while/body/jit(dynamic_update_index_in_dim)/dynamic_update_slice | solution.py:194
  445.2 15.1 %dynamic_update_slice.34 = f32[2,680,4,64]{1,0,3,2:T(2,128)} dynamic-update-slice(f32[2,680,4,64]{1,0,3,2:T(2,128)} %get-tuple-element.506, f32[1,680,4,64]{1,0,3,2:T(1,128)} %copy.159, s32[]{:T(128)S(6)} %copy.181, s32[]{:T(128)} %constant.72.clone.1..sunk, s32[]{:T(128)} %constant.72.clone.1..sunk, s32[]{:T(128)} %constant.72.clone.1..sunk) | dynamic-update-slice | bytes 1392644 | tf_op jit(solution)/shard_map/while/body/jit(dynamic_update_index_in_dim)/dynamic_update_slice | solution.py:194
  460.3 5.1 multiply_reduce_fusion.5
  465.5 5.0 fusion.74
  470.5 3.0 stack.25
  473.5 2.2 copy.105
  475.7 3.3 copy.115
  479.1 3.1 reshape.346
  482.2 3.0 stack.26
  485.2 2.2 copy.106
  487.4 6.9 fusion.94
  494.8 8.3 fusion.106
  503.1 9.0 fusion.91
  514.1 4.4 fusion.93
  518.5 173.9 %all-reduce.15.cloned.1.call-done = (f32[2,680,1024]{2,1,0:T(8,128)}, f32[2,680,1024]{2,1,0:T(8,128)}) async-done(((f32[2,680,1024]{2,1,0:T(8,128)}, f32[2,680,1024]{2,1,0:T(8,128)}), (f32[2,680,1024]{2,1,0:T(8,128)}, f32[2,680,1024]{2,1,0:T(8,128)})) %all-reduce.15.cloned.1.call-update) | async-done | bytes 11141136 | tf_op jit(solution)/shard_map/psum | solution.py:131
  692.4 4.8 fusion.95
  698.2 2.8 fusion.61
  701.1 12.1 fusion.72
  713.3 3.7 fusion.89
  721.2 40.4 %all-reduce.1 = (f32[16]{0:T(128)S(1)}, f32[6144]{0:T(1024)}, f32[2,256]{1,0:T(2,128)}, f32[4]{0:T(128)}, f32[1024]{0:T(1024)}, /*index=5*/f32[1024]{0:T(1024)}, f32[1024]{0:T(1024)}) all-reduce(f32[16]{0:T(128)S(1)} %convert_dynamic-update-slice_fusion, f32[6144]{0:T(1024)S(1)} %reduce_sum.288, ...), channel_id=1, replica_groups=mesh['dp'=8,'mp'=4] {'dp'}, use_global_device_ids=true, to_apply=%add | all-reduce | flops 9748 | bytes 77984
  762.5 27.4 %all-gather = f32[8,2,256]{2,1,0:T(2,128)S(1)} all-gather(f32[1,2,256]{2,1,0:T(2,128)S(1)} %fusion.87), channel_id=1, replica_groups=mesh['dp'=8,'mp'=4] {'dp'}, dimensions={0}, use_global_device_ids=true | all-gather | bytes 18432 | tf_op jit(solution)/shard_map/all_gather | solution.py:235
  791.6 499.6 %all-reduce.13.cloned.1.call-done = (f32[256,6144]{1,0:T(8,128)}, f32[1024,3,256]{2,0,1:T(8,128)}, f32[256,1024]{1,0:T(8,128)}, f32[1024,1024]{1,0:T(8,128)}, f32[1024,1024]{1,0:T(8,128)}) async-done(((f32[256,6144]{1,0:T(8,128)}, f32[1024,3,256]{2,0,1:T(8,128)}, f32[256,1024]{1,0:T(8,128)}, f32[1024,1024]{1,0:T(8,128)}, f32[1024,1024]{1,0:T(8,128)}), (f32[256,6144]{1,0:T(8,128)}, ...) | async-done | bytes 18874384 | tf_op jit(solution)/shard_map/psum | solution.py:242
  1291.3 6.3 copy.202
  (274 shorter events, 58.4 us)
Async XLA Ops:
  7.2 6.7 copy-start
  7.2 6.1 copy-start.73
  7.2 20.5 %copy-start.52 = (f32[6144]{0:T(1024)S(1)}, f32[6144]{0:T(1024)}, u32[]{:S(2)}) copy-start(f32[6144]{0:T(1024)} %param.28) | copy-start | bytes 73732
  7.2 193.4 %all-reduce.9.cloned.1.call-start = ((), (), s32[]{:S(2)}) async-start(), calls=%async_computation | async-start | bytes 11141120 | tf_op jit(solution)/shard_map/psum | solution.py:119
  7.3 6.0 copy-start.71
  10.6 20.5 %copy-start.40 = (f32[2,680]{1,0:T(2,128)}, f32[2,680]{1,0:T(2,128)S(1)}, u32[]{:S(2)}) copy-start(f32[2,680]{1,0:T(2,128)S(1)} %broadcast_multiply_fusion.1) | copy-start | bytes 16324
  13.3 23.7 %copy-start.44 = (f32[2,680]{1,0:T(2,128)}, f32[2,680]{1,0:T(2,128)S(1)}, u32[]{:S(2)}) copy-start(f32[2,680]{1,0:T(2,128)S(1)} %fusion.83) | copy-start | bytes 16324
  27.8 4.8 copy-start.70
  42.7 13.1 copy-start.75
  42.7 13.1 copy-start.65
  52.9 9.8 copy-start.34
  52.9 9.8 copy-start.36
  52.9 9.8 copy-start.66
  52.9 9.8 copy-start.67
  55.8 7.1 copy-start.61
  55.9 6.8 copy-start.32
  56.0 6.9 copy-start.38
  92.3 108.4 %copy-start.55 = (f32[1024]{0:T(1024)S(1)}, f32[1024]{0:T(1024)}, u32[]{:S(2)}) copy-start(f32[1024]{0:T(1024)} %param.33) | copy-start | bytes 12292
  92.3 240.1 %all-reduce.11.cloned.1.call-start = ((), (), s32[]{:S(2)}) async-start(), calls=%async_computation.1 | async-start | bytes 11141120 | tf_op jit(solution)/shard_map/psum | solution.py:152
  92.4 112.7 %copy-start.46 = (f32[2,1024]{1,0:T(2,128)}, f32[2,1024]{1,0:T(2,128)S(1)}, u32[]{:S(2)}) copy-start(f32[2,1024]{1,0:T(2,128)S(1)} %get-tuple-element.337) | copy-start | bytes 24580
  207.6 4.3 copy-start.24
  212.0 7.3 copy-start.79
  219.3 4.9 copy-start.78
  224.2 468.2 %all-reduce.15.cloned.1.call-start = ((), (), s32[]{:S(2)}) async-start(), calls=%async_computation.3 | async-start | bytes 22282240 | tf_op jit(solution)/shard_map/psum | solution.py:131
  332.4 17.8 %copy-start.8 = (f32[2,680,1024]{2,1,0:T(8,128)S(1)}, f32[2,680,1024]{2,1,0:T(8,128)}, u32[]{:S(2)}) copy-start(f32[2,680,1024]{2,1,0:T(8,128)} %all-reduce.11.cloned.1.call-done) | copy-start | bytes 16711684
  353.9 3.9 copy-start.31
  366.1 94.2 %copy-start.33 = (f32[2,680,4]{1,0,2:T(2,128)S(1)}, f32[2,680,4]{1,0,2:T(2,128)}, u32[]{:S(2)}) copy-start(f32[2,680,4]{1,0,2:T(2,128)} %copy-done.32) | copy-start | bytes 65284
  366.1 94.2 %copy-start.62 = (f32[4]{0:T(128)S(1)}, f32[4]{0:T(128)}, u32[]{:S(2)}) copy-start(f32[4]{0:T(128)} %copy-done.61) | copy-start | bytes 52
  366.1 4.0 copy-start.11
  413.2 4.0 copy-start.11
  460.3 5.1 copy-start.37
  460.3 5.2 copy-start.35
  460.3 5.2 copy-start.12
  460.3 5.2 copy-start.13
  460.3 5.2 copy-start.39
  494.3 796.9 %all-reduce.13.cloned.1.call-start = ((), (), s32[]{:S(2)}) async-start(), calls=%async_computation.2 | async-start | bytes 37748736 | tf_op jit(solution)/shard_map/psum | solution.py:242
  494.8 8.3 copy-start.21
  503.0 9.1 copy-start.14
  503.0 9.1 copy-start.23
  503.0 11.0 copy-start.19
  503.0 11.0 copy-start.25
  503.1 11.0 copy-start.26
  503.1 11.0 copy-start.27
  514.1 178.3 %copy-start.41 = (f32[2,680]{1,0:T(2,128)S(1)}, f32[2,680]{1,0:T(2,128)}, u32[]{:S(2)}) copy-start(f32[2,680]{1,0:T(2,128)} %copy-done.40) | copy-start | bytes 16324
  514.1 178.3 %copy-start.43 = (f32[2,1024]{1,0:T(2,128)S(1)}, f32[2,1024]{1,0:T(2,128)}, u32[]{:S(2)}) copy-start(f32[2,1024]{1,0:T(2,128)} %copy-done.42) | copy-start | bytes 24580
  518.5 178.7 %copy-start.51 = (f32[2,680]{1,0:T(2,128)S(1)}, f32[2,680]{1,0:T(2,128)}, u32[]{:S(2)}) copy-start(f32[2,680]{1,0:T(2,128)} %copy-done.50) | copy-start | bytes 16324
  518.5 178.8 %copy-start.45 = (f32[2,680]{1,0:T(2,128)S(1)}, f32[2,680]{1,0:T(2,128)}, u32[]{:S(2)}) copy-start(f32[2,680]{1,0:T(2,128)} %copy-done.44) | copy-start | bytes 16324
  692.4 4.9 copy-start.2
  692.4 5.9 copy-start.5
  692.4 8.6 slice-start
  697.2 3.9 copy-start.47
  697.2 3.9 copy-start.49
  697.2 3.9 copy-start.56
  697.2 3.9 copy-start.63
  701.1 12.2 copy-start.60
  701.1 12.2 copy-start.59
  701.1 12.2 copy-start.54
  717.1 4.0 copy-start.76
  717.1 4.1 copy-start.57
  717.1 4.1 copy-start.58
  717.1 4.1 copy-start.64
  1291.2 6.3 copy-start.17
  1297.6 4.0 copy-start.16
  1299.5 4.1 copy-start.15
  (29 other events, 55.5 us)
Sparse Core Ops, SparseCore 0:
  92.5 108.1 all-reduce.8
  224.3 108.0 all-reduce.10
  494.4 197.8 all-reduce.14
  717.2 573.9 all-reduce.12
where the time goes:
time: 1330 us; the launch traced here: 1310 us
  waiting for transfers between devices  876 us (66%)
  local copies, waits for them, and re-layouts  145 us (11%)
  matrix products  103 us (8%)
  other arithmetic  91.4 us (7%)
  blocking collectives  81 us (6%)
  between operations  15.7 us (1%)
    psum x1, waiting for transfers between devices, shards(): lax.psum((ada_weight_grad, ada_bias_grad, qkv_weight_grad, qv_bias_grad,...  500 us
    psum x1, waiting for transfers between devices, shards(): lax.psum(jnp.dot(hidden_low, fc2_weight, preferred_element_type=jnp.float...  174 us
    psum x1, waiting for transfers between devices, shards(): lax.psum(jnp.dot(mixed_flat, proj_weight, preferred_element_type=jnp.floa...  103 us
    psum x1, waiting for transfers between devices, shards(): lax.psum(jnp.einsum('rf,df->rd', upper_grad, fc1_weight, preferred_elemen...  98.7 us
    dynamic_update_slice x8, local copies, waits for them, and re-layouts, shards(): lax.map(attend_back, (query_low, key_low, value_low, mixed_grad, log_tota...  67.2 us
    unnamed x1, blocking collectives  40.4 us
    unnamed x170, local copies, waits for them, and re-layouts  30.3 us
    all_gather x1, blocking collectives, shards(): lax.all_gather(class_grad, 'dp', axis=0, tiled=True)  27.4 us
  transfers between devices with their start and end apart: 4, of which 4 were waited for; matrix products, arithmetic and copies ran while one was open for 3% of the time, Pallas kernels for 0%

commit v1 on v0

v1 whole, which is shorter than its diff:
```python
import functools

import jax
import jax.numpy as jnp
import numpy as np
from jax import lax
from jax.experimental import pallas as pl
from jax.experimental.pallas import tpu as pltpu
from jax.sharding import PartitionSpec as P

SIDE_LIST = (1, 2, 3, 4, 5, 6, 8, 10, 13, 16)
EPSILON = 1e-06
MESH = pl.DeviceIdType.MESH
F32, BF16 = jnp.float32, jnp.bfloat16
GELU_C = 0.7978845608028654
GELU_A = 0.044715
LN_TILE = 64
NT = (((1,), (1,)), ((), ()))
TN = (((0,), (0,)), ((), ()))
NN = (((1,), (0,)), ((), ()))
ATT, DS, DF, BR = 0, 2, 4, 6


def dot(a, b, dims=NN):
    return lax.dot_general(a, b, dims, preferred_element_type=F32)


def norm_rows(v):
    center = v - jnp.mean(v, axis=-1, keepdims=True)
    scale = lax.rsqrt(jnp.mean(center * center, axis=-1, keepdims=True) + EPSILON)
    return center * scale, scale


def fold(v):
    return jnp.sum(v.reshape(v.shape[0] // 8, 8, v.shape[1]), axis=0)


def head_sum(v, blocks):
    high = v.astype(BF16)
    rest = (v - high.astype(F32)).astype(BF16)
    return dot(high, blocks) + dot(rest, blocks)


def block_kernel(
    slots,
    mod_part, ada_b, tok_hbm, cot_hbm, stops, lim_hbm,
    qkvw_hbm, projw_hbm, fc1w_hbm, fc2w_hbm,
    qv_b, es_row, proj_b, fc1_b, fc2_b,
    out_hbm, tg_hbm, g1_hbm, g2_hbm, gp_hbm, gq_hbm, modg_out, small_out,
    tok, cot, fst, sec, dbr, hid, dup,
    att, dst, dfr,
    qk, qkn, mix, dmx, acc,
    rs_buf, y_buf,
    qkvw, projw, fc1w, fc2w, lim,
    stage, modr, mod, g2r, fb1, lanes,
    in_sem, out_sem, stage_sem,
    mod_s, mod_r, g2_s, g2_r, rs_s, rs_r, y_s, y_r, ag_s, ag_r,
):
    items, padded, width = tok.shape
    half = width // 2
    me = lax.axis_index("mp")
    core = lax.rem(me, 2)
    core_mate = me + 1 - 2 * core
    y_mate = lax.rem(me + 2, 4)
    n_ln = padded // LN_TILE
    mt = padded // 2

    def rows_of(t, n):
        return pl.ds(pl.multiple_of(t * n, n), n)

    loads = {}
    for k, (name, src, to) in enumerate((
        ("tok", tok_hbm, tok), ("qkvw", qkvw_hbm, qkvw), ("lim", lim_hbm, lim),
        ("projw", projw_hbm, projw), ("cot", cot_hbm, cot),
        ("fc1w", fc1w_hbm, fc1w), ("fc2w", fc2w_hbm, fc2w),
    )):
        loads[name] = pltpu.make_async_copy(src, to, in_sem.at[k])
        loads[name].start()

    barrier = pltpu.get_barrier_semaphore()
    for step in (1, 2, 3):
        pl.semaphore_signal(barrier, inc=1, device_id={"mp": lax.rem(me + step, 4)}, device_id_type=MESH)
    pl.semaphore_wait(barrier, 3)

    def share(buf, send, recv):
        copies = []
        for step in (1, 2, 3):
            copies.append(pltpu.make_async_remote_copy(
                src_ref=buf.at[me], dst_ref=buf.at[me], send_sem=send.at[step - 1], recv_sem=recv.at[step - 1],
                device_id={"mp": lax.rem(me + step, 4)}, device_id_type=MESH))
        for copy in copies:
            copy.start()
        return copies

    modr[me] = mod_part[...]
    sent = share(modr, mod_s, mod_r)
    for copy in sent:
        copy.wait()
    mod[...] = ((modr[0] + modr[1]) + (modr[2] + modr[3])) + ada_b[...]

    def vec(i, k):
        return mod[i, k:k + 1, :]

    def rs_copy(buf, i, k):
        return pltpu.make_async_remote_copy(
            src_ref=buf.at[i, 1 - core, pl.ds(0, slots)], dst_ref=rs_buf.at[i], send_sem=rs_s.at[k + i], recv_sem=rs_r.at[k + i],
            device_id={"mp": core_mate}, device_id_type=MESH)

    def y_copy(buf, i, k):
        dst = dfr.at[i, 0, pl.ds(0, slots)] if k == DS else y_buf.at[i]
        return pltpu.make_async_remote_copy(
            src_ref=buf.at[i, core, pl.ds(0, slots)], dst_ref=dst, send_sem=y_s.at[k + i], recv_sem=y_r.at[k + i],
            device_id={"mp": y_mate}, device_id_type=MESH)

    def ag_copy(buf, i, k):
        return pltpu.make_async_remote_copy(
            src_ref=buf.at[i, core, pl.ds(0, slots)], dst_ref=buf.at[i, core, pl.ds(0, slots)],
            send_sem=ag_s.at[k + i], recv_sem=ag_r.at[k + i],
            device_id={"mp": core_mate}, device_id_type=MESH)

    add_rows = slots // 5

    def rs_finish(buf, i, k):
        rs_copy(buf, i, k).wait()

        def add(t, _):
            rows = rows_of(t, add_rows)
            buf[i, core, rows, :] = buf[i, core, rows, :] + rs_buf[i, rows, :]
            return 0
        lax.fori_loop(0, 5, add, 0)

    def y_finish(buf, i, k):
        y_copy(buf, i, k).wait()

        def add(t, _):
            rows = rows_of(t, add_rows)
            other = dfr[i, 0, rows, :] if k == DS else y_buf[i, rows, :]
            buf[i, core, rows, :] = buf[i, core, rows, :] + other
            return 0
        lax.fori_loop(0, 5, add, 0)

    def wide(buf, i, rows):
        return jnp.concatenate([buf[i, 0, rows, :], buf[i, 1, rows, :]], axis=1)

    def put_wide(buf, i, rows, v):
        buf[i, 0, rows, :] = v[:, :half]
        buf[i, 1, rows, :] = v[:, half:]

    def blocks_of(n):
        a = lax.broadcasted_iota(jnp.int32, (n, n), 0) // 64
        b = lax.broadcasted_iota(jnp.int32, (n, n), 1) // 64
        return jnp.where(a == b, 1.0, 0.0).astype(BF16)

    ends = np.cumsum(np.array([s * s for s in SIDE_LIST]))
    tiles = ((0, 240, 1, 256), (240, 176, 1, 512), (416, 96, 3, padded))

    def keep_of(i, rows, keys):
        live = jnp.int32(0)
        for s in range(len(SIDE_LIST)):
            live = jnp.where(stops[i] == s + 1, int(ends[s]), live)
        bound = jnp.minimum(lim[rows, :], live)
        n = bound.shape[0]
        return lax.broadcasted_iota(jnp.int32, (n, keys), 1) < bound[:, 0:1]

    def head_lanes(shape, h):
        return (lax.broadcasted_iota(jnp.int32, shape, 1) // 64) == h

    def mask_head(v, h):
        return jnp.where(head_lanes(v.shape, h), v.astype(F32), 0.0).astype(BF16)

    def each_tile(body):
        for first_row, n, steps, keys in tiles:
            if steps == 1:
                body(pl.ds(first_row, n), keys)
            else:
                def step(t, _, first_row=first_row, n=n, keys=keys):
                    body(pl.ds(pl.multiple_of(first_row + t * n, 16), n), keys)
                    return 0
                lax.fori_loop(0, steps, step, 0)

    def first_norm(i):
        def body(t, _):
            rows = rows_of(t, LN_TILE)
            n, _r = norm_rows(tok[i, rows, :].astype(F32))
            fst[i, rows, :] = (n * (1.0 + vec(i, 2)) + vec(i, 4)).astype(BF16)
            return 0
        lax.fori_loop(0, n_ln, body, 0)

    def project(i):
        blocks = blocks_of(256)

        def body(t, _):
            rows = rows_of(t, mt)
            f = fst[i, rows, :]
            q = dot(f, qkvw[0]) + qv_b[0:1, :]
            qk[i, 0, rows, :] = q
            u = q * lax.rsqrt(head_sum(q * q, blocks) + EPSILON) * es_row[...]
            qkn[i, 0, 0, rows, :] = u[:, :128].astype(BF16)
            qkn[i, 0, 1, rows, :] = u[:, 128:].astype(BF16)
            k = dot(f, qkvw[1])
            qk[i, 1, rows, :] = k
            u = k * lax.rsqrt(head_sum(k * k, blocks) + EPSILON)
            qkn[i, 1, 0, rows, :] = u[:, :128].astype(BF16)
            qkn[i, 1, 1, rows, :] = u[:, 128:].astype(BF16)
            v = dot(f, qkvw[2]) + qv_b[1:2, :]
            qkn[i, 2, 0, rows, :] = v[:, :128].astype(BF16)
            qkn[i, 2, 1, rows, :] = v[:, 128:].astype(BF16)
            return 0
        lax.fori_loop(0, 2, body, 0)

    def attend(i):
        def slab_body(slab, _):
            def body(rows, keys):
                keep = keep_of(i, rows, keys)
                total = None
                for h in (0, 1):
                    s = dot(qkn[i, 0, slab, rows, :], mask_head(qkn[i, 1, slab, pl.ds(0, keys), :], h), NT)
                    e = jnp.where(keep, jnp.exp(s), 0.0)
                    p = (e * (1.0 / jnp.sum(e, axis=-1, keepdims=True))).astype(BF16)
                    o = dot(p, mask_head(qkn[i, 2, slab, pl.ds(0, keys), :], h))
                    total = o if total is None else total + o
                mix[i, slab, rows, :] = total.astype(BF16)
            each_tile(body)
            return 0
        lax.fori_loop(0, 2, slab_body, 0)

    def attend_out(i):
        def body(t, _):
            rows = rows_of(t, mt)
            m = jnp.concatenate([mix[i, 0, rows, :], mix[i, 1, rows, :]], axis=1)
            for h in (0, 1):
                att[i, h, rows, :] = dot(m, projw[:, h * half:(h + 1) * half])
            return 0
        lax.fori_loop(0, 2, body, 0)

    def mlp(i):
        def body(t, total):
            rows = rows_of(t, LN_TILE)
            middle = tok[i, rows, :].astype(F32) + vec(i, 0) * (wide(att, i, rows) + proj_b[...])
            n, _r = norm_rows(middle)
            sec[i, rows, :] = (n * (1.0 + vec(i, 3)) + vec(i, 5)).astype(BF16)
            d = (cot[i, rows, :].astype(F32) * vec(i, 1)).astype(BF16)
            dbr[i, rows, :] = d
            return total + fold(d.astype(F32))
        total = lax.fori_loop(0, n_ln, body, jnp.zeros((8, width), F32))
        small_out[0:1, :] = small_out[0:1, :] + jnp.sum(total, axis=0, keepdims=True)

        def column(j, _):
            cols = pl.ds(pl.multiple_of(j * 256, 256), 256)

            def body(t, _):
                rows = rows_of(t, mt)
                u = dot(sec[i, rows, :], fc1w[:, cols]) + fc1_b[j]
                dh = dot(dbr[i, rows, :], fc2w[cols, :], NT)
                th = jnp.tanh(GELU_C * (u + GELU_A * u * u * u))
                hid[i, rows, cols] = (0.5 * u * (1.0 + th)).astype(BF16)
                slope = 0.5 * (1.0 + th) + 0.5 * u * (1.0 - th * th) * (GELU_C + (3.0 * GELU_C * GELU_A) * u * u)
                d = (dh * slope).astype(BF16)
                dup[i, j, rows, :] = d
                fb1[j] = fb1[j] + fold(d.astype(F32))
                return 0
            lax.fori_loop(0, 2, body, 0)
            return 0
        lax.fori_loop(0, dup.shape[1], column, 0)

        def back(t, _):
            rows = rows_of(t, mt)
            d = jnp.concatenate([dup[i, j, rows, :] for j in range(dup.shape[1])], axis=1)
            for h in (0, 1):
                dst[i, h, rows, :] = dot(d, fc1w[h * half:(h + 1) * half, :], NT)
            return 0
        lax.fori_loop(0, 2, back, 0)

    def stage_out(slot, hbm, j):
        return pltpu.make_async_copy(stage.at[slot], hbm.at[rows_of(j, 256)], stage_sem.at[slot])

    def fc_grads():
        def pair(lhs, rhs, slot, hbm, j):
            cols = pl.ds(pl.multiple_of(j * 256, 256), 256)

            def piece(n, _):
                to = pl.ds(pl.multiple_of(n * 256, 256), 256)
                stage[slot, :, to] = dot(lhs[0, :, cols], rhs(0, n), TN) + dot(lhs[1, :, cols], rhs(1, n), TN)
                return 0
            lax.fori_loop(0, width // 256, piece, 0)
            stage_out(slot, hbm, j).start()

        def body(j, _):
            @pl.when(j > 0)
            def _():
                stage_out(0, g2_hbm, j - 1).wait()
            pair(hid, lambda i, n: dbr[i, :, pl.ds(pl.multiple_of(n * 256, 256), 256)], 0, g2_hbm, j)

            @pl.when(j > 0)
            def _():
                stage_out(1, g1_hbm, j - 1).wait()
            pair(sec, lambda i, n: dup[i, n], 1, g1_hbm, j)
            return 0
        lax.fori_loop(0, 4, body, 0)
        stage_out(0, g2_hbm, 3).wait()
        stage_out(1, g1_hbm, 3).wait()

    def second_back(i):
        zero = jnp.zeros((8, width), F32)

        def body(t, sums):
            rows = rows_of(t, LN_TILE)
            attended = wide(att, i, rows) + proj_b[...]
            n, r = norm_rows(tok[i, rows, :].astype(F32) + vec(i, 0) * attended)
            dy = wide(dst, i, rows)
            dn = dy * (1.0 + vec(i, 3))
            dm = cot[i, rows, :].astype(F32) + r * (
                dn - jnp.mean(dn, axis=-1, keepdims=True) - n * jnp.mean(dn * n, axis=-1, keepdims=True))
            put_wide(dst, i, rows, dm)
            da = (dm * vec(i, 0)).astype(BF16)
            sec[i, rows, :] = da
            return (sums[0] + fold(dm * attended), sums[1] + fold(dy * n), sums[2] + fold(dy), sums[3] + fold(da.astype(F32)))
        sums = lax.fori_loop(0, n_ln, body, (zero, zero, zero, zero))
        for k, s in zip((0, 3, 5), sums[:3]):
            modg_out[i, k:k + 1, :] = jnp.sum(s, axis=0, keepdims=True)
        small_out[2:3, :] = small_out[2:3, :] + jnp.sum(sums[3], axis=0, keepdims=True)

        def mixed(t, _):
            rows = rows_of(t, mt)
            d = dot(sec[i, rows, :], projw[...], NT)
            dmx[0, rows, :] = d[:, :128].astype(BF16)
            dmx[1, rows, :] = d[:, 128:].astype(BF16)
            return 0
        lax.fori_loop(0, 2, mixed, 0)

    def attend_back(i):
        blocks = blocks_of(128)

        def slab_body(slab, _):
            acc[...] = jnp.zeros_like(acc)

            def body(rows, keys):
                keep = keep_of(i, rows, keys)
                kr = pl.ds(0, keys)
                for h in (0, 1):
                    km = mask_head(qkn[i, 1, slab, kr, :], h)
                    s = dot(qkn[i, 0, slab, rows, :], km, NT)
                    e = jnp.where(keep, jnp.exp(s), 0.0)
                    p = e * (1.0 / jnp.sum(e, axis=-1, keepdims=True))
                    dom = mask_head(dmx[slab, rows, :], h)
                    acc[2, kr, :] += dot(p.astype(BF16), dom, TN)
                    dp = dot(dom, qkn[i, 2, slab, kr, :], NT)
                    ds = (p * (dp - jnp.sum(dp * p, axis=-1, keepdims=True))).astype(BF16)
                    acc[0, rows, :] += dot(ds, km)
                    acc[1, kr, :] += dot(ds, mask_head(qkn[i, 0, slab, rows, :], h), TN)
            each_tile(body)

            es = jnp.where(slab == 0, es_row[:, :128], es_row[:, 128:])

            def close(t, sums):
                rows = rows_of(t, LN_TILE)

                def unit(c, g):
                    pre = qk[i, c, rows, pl.ds(pl.multiple_of(slab * 128, 128), 128)]
                    r = lax.rsqrt(head_sum(pre * pre, blocks) + EPSILON)
                    u = pre * r
                    gu = g * u
                    return r * (g - u * head_sum(gu, blocks)), gu
                dq, gu = unit(0, acc[0, rows, :] * es)
                dk, _g = unit(1, acc[1, rows, :])
                dq, dk, dv = dq.astype(BF16), dk.astype(BF16), acc[2, rows, :].astype(BF16)
                to = pl.ds(pl.multiple_of(slab * 128, 128), 128)
                dup[i, 0, rows, to] = dq
                dup[i, 1, rows, to] = dk
                dup[i, 2, rows, to] = dv
                return sums[0] + fold(dq.astype(F32)), sums[1] + fold(dv.astype(F32)), sums[2] + fold(gu)
            zero = jnp.zeros((8, 128), F32)
            sums = lax.fori_loop(0, n_ln, close, (zero, zero, zero))
            for k in range(3):
                lanes[k, slab] = lanes[k, slab] + sums[k]
            return 0
        lax.fori_loop(0, 2, slab_body, 0)

    def first_grad(i):
        def body(t, _):
            rows = rows_of(t, mt)
            for h in (0, 1):
                total = None
                for c in range(3):
                    o = dot(dup[i, c, rows, :], qkvw[c, h * half:(h + 1) * half, :], NT)
                    total = o if total is None else total + o
                dfr[i, h, rows, :] = total
            return 0
        lax.fori_loop(0, 2, body, 0)

    def attention_grads():
        def piece(n, _):
            to = pl.ds(pl.multiple_of(n * 512, 512), 512)
            for slab in (0, 1):
                stage[0, slab * 128:(slab + 1) * 128, to] = (
                    dot(mix[0, slab], sec[0, :, to], TN) + dot(mix[1, slab], sec[1, :, to], TN))
            return 0
        lax.fori_loop(0, 2, piece, 0)
        to_proj = pltpu.make_async_copy(stage.at[0], gp_hbm, stage_sem.at[0])
        to_proj.start()
        to_proj.wait()

        def part(c, j):
            return pltpu.make_async_copy(
                stage.at[1, :, pl.ds(pl.multiple_of(c * 256, 256), 256)], gq_hbm.at[c, rows_of(j, 256)], stage_sem.at[1])

        def body(n, _):
            j, c = n // 3, lax.rem(n, 3)
            cols = pl.ds(pl.multiple_of(j * 256, 256), 256)
            to = pl.ds(pl.multiple_of(c * 256, 256), 256)
            total = None
            for i in (0, 1):
                o = dot(fst[i, :, cols], dup[i, c], TN)
                total = o if total is None else total + o
            stage[1, :, to] = total
            part(c, j).start()
            part(c, j).wait()
            return 0
        lax.fori_loop(0, 12, body, 0)

    def first_back(i):
        zero = jnp.zeros((8, width), F32)

        def body(t, sums):
            rows = rows_of(t, LN_TILE)
            n, r = norm_rows(tok[i, rows, :].astype(F32))
            dy = wide(dfr, i, rows)
            dn = dy * (1.0 + vec(i, 2))
            g = wide(dst, i, rows) + r * (
                dn - jnp.mean(dn, axis=-1, keepdims=True) - n * jnp.mean(dn * n, axis=-1, keepdims=True))
            fst[i, rows, :] = g.astype(BF16)
            return sums[0] + fold(dy * n), sums[1] + fold(dy)
        sums = lax.fori_loop(0, n_ln, body, (zero, zero))
        for k, s in zip((2, 4), sums):
            modg_out[i, k:k + 1, :] = jnp.sum(s, axis=0, keepdims=True)
        pltpu.make_async_copy(fst.at[i], tg_hbm.at[i], out_sem.at[i]).start()

    def branch(i):
        def body(t, _):
            rows = rows_of(t, mt)
            for h in (0, 1):
                dst[i, h, rows, :] = dot(hid[i, rows, :], fc2w[:, h * half:(h + 1) * half])
            return 0
        lax.fori_loop(0, 2, body, 0)

        def sums_of(t, sums):
            rows = rows_of(t, LN_TILE)
            g = cot[i, rows, :].astype(F32)
            return sums[0] + fold(g * wide(dst, i, rows)), sums[1] + fold(g)
        zero = jnp.zeros((8, width), F32)
        sums = lax.fori_loop(0, n_ln, sums_of, (zero, zero))
        g2r[me, i:i + 1, :] = jnp.sum(sums[0], axis=0, keepdims=True)
        modg_out[i, 1:2, :] = fc2_b[...] * jnp.sum(sums[1], axis=0, keepdims=True)

    def block_end(i):
        def body(t, _):
            rows = rows_of(t, LN_TILE)
            middle = tok[i, rows, :].astype(F32) + vec(i, 0) * (wide(att, i, rows) + proj_b[...])
            cot[i, rows, :] = (middle + vec(i, 1) * (wide(dst, i, rows) + fc2_b[...])).astype(BF16)
            return 0
        lax.fori_loop(0, n_ln, body, 0)
        pltpu.make_async_copy(cot.at[i], out_hbm.at[i], out_sem.at[2 + i]).start()

    small_out[...] = jnp.zeros_like(small_out)
    modg_out[...] = jnp.zeros_like(modg_out)
    fb1[...] = jnp.zeros_like(fb1)
    lanes[...] = jnp.zeros_like(lanes)
    g2r[...] = jnp.zeros_like(g2r)
    loads["tok"].wait()
    for i in (0, 1):
        first_norm(i)
        if i == 0:
            loads["qkvw"].wait()
        project(i)
        if i == 0:
            loads["lim"].wait()
        attend(i)
        if i == 0:
            loads["projw"].wait()
        attend_out(i)
        rs_copy(att, i, ATT).start()
        rs_finish(att, i, ATT)
        if i == 0:
            y_copy(att, 0, ATT).start()
    for name in ("cot", "fc1w", "fc2w"):
        loads[name].wait()

    y_finish(att, 0, ATT)
    y_copy(att, 1, ATT).start()
    ag_copy(att, 0, ATT).start()
    ag_copy(att, 0, ATT).wait()
    mlp(0)
    rs_copy(dst, 0, DS).start()
    rs_finish(dst, 0, DS)

    y_finish(att, 1, ATT)
    y_copy(dst, 0, DS).start()
    ag_copy(att, 1, ATT).start()
    ag_copy(att, 1, ATT).wait()
    mlp(1)
    rs_copy(dst, 1, DS).start()
    fc_grads()
    rs_finish(dst, 1, DS)

    for i in (0, 1):
        y_finish(dst, i, DS)
        if i == 0:
            y_copy(dst, 1, DS).start()
        else:
            y_copy(dfr, 0, DF).start()
        ag_copy(dst, i, DS).start()
        ag_copy(dst, i, DS).wait()
        second_back(i)
        attend_back(i)
        first_grad(i)
        rs_copy(dfr, i, DF).start()
        rs_finish(dfr, i, DF)
    attention_grads()

    for i in (0, 1):
        y_finish(dfr, i, DF)
        if i == 0:
            y_copy(dfr, 1, DF).start()
        else:
            y_copy(dst, 0, BR).start()
        ag_copy(dfr, i, DF).start()
        ag_copy(dfr, i, DF).wait()
        first_back(i)
        branch(i)
        rs_copy(dst, i, BR).start()
        rs_finish(dst, i, BR)

    sent = share(g2r, g2_s, g2_r)
    for copy in sent:
        copy.wait()
    total = (g2r[0] + g2r[1]) + (g2r[2] + g2r[3])
    for i in (0, 1):
        modg_out[i, 1:2, :] = modg_out[i, 1:2, :] + total[i:i + 1, :]
    for j in range(4):
        small_out[1:2, j * 256:(j + 1) * 256] = jnp.sum(fb1[j], axis=0, keepdims=True)
    for k in range(3):
        for slab in (0, 1):
            at = k * 256 + slab * 128
            small_out[3:4, at:at + 128] = jnp.sum(lanes[k, slab], axis=0, keepdims=True)

    for i in (0, 1):
        y_finish(dst, i, BR)
        if i == 0:
            y_copy(dst, 1, BR).start()
        ag_copy(dst, i, BR).start()
        ag_copy(dst, i, BR).wait()
        block_end(i)
    for i in (0, 1):
        pltpu.make_async_copy(fst.at[i], tg_hbm.at[i], out_sem.at[i]).wait()
        pltpu.make_async_copy(cot.at[i], out_hbm.at[i], out_sem.at[2 + i]).wait()


def run_block(mod_part, ada_b, tok, cot, stops, qkvw, projw, fc1w, fc2w, qv_b, es_row, proj_b, fc1_b, fc2_b, slots):
    items, padded, width = tok.shape
    half = width // 2
    hidden = fc1w.shape[1]
    ends = np.cumsum(np.array([s * s for s in SIDE_LIST]))
    level = np.minimum(np.searchsorted(ends, np.arange(padded), side="right"), len(SIDE_LIST) - 1)
    lim = jnp.asarray(np.broadcast_to(ends[level][:, None], (padded, 128)), jnp.int32)
    hbm = pl.BlockSpec(memory_space=pl.ANY)
    vmem = pl.BlockSpec(memory_space=pltpu.VMEM)
    smem = pl.BlockSpec(memory_space=pltpu.SMEM)
    wide_b = (items, padded, width)
    wide_f = (items, 2, padded, half)
    dma = pltpu.SemaphoreType.DMA
    return pl.pallas_call(
        functools.partial(block_kernel, slots),
        out_shape=(
            jax.ShapeDtypeStruct(wide_b, BF16), jax.ShapeDtypeStruct(wide_b, BF16),
            jax.ShapeDtypeStruct((width, hidden), F32), jax.ShapeDtypeStruct((hidden, width), F32),
            jax.ShapeDtypeStruct(projw.shape, F32), jax.ShapeDtypeStruct(qkvw.shape, F32),
            jax.ShapeDtypeStruct((items, 8, width), F32), jax.ShapeDtypeStruct((8, width), F32),
        ),
        in_specs=[vmem, vmem, hbm, hbm, smem, hbm, hbm, hbm, hbm, hbm, vmem, vmem, vmem, vmem, vmem],
        out_specs=(hbm, hbm, hbm, hbm, hbm, hbm, vmem, vmem),
        scratch_shapes=[
            *[pltpu.VMEM(wide_b, BF16) for _ in range(5)],
            pltpu.VMEM((items, padded, hidden), BF16), pltpu.VMEM((items, hidden // 256, padded, 256), BF16),
            *[pltpu.VMEM(wide_f, F32) for _ in range(3)],
            pltpu.VMEM((items, 2, padded, 256), F32),
            pltpu.VMEM((items, 3, 2, padded, 128), BF16),
            pltpu.VMEM((items, 2, padded, 128), BF16),
            pltpu.VMEM((2, padded, 128), BF16),
            pltpu.VMEM((3, padded, 128), F32),
            pltpu.VMEM((items, slots, half), F32),
            pltpu.VMEM((items, slots, half), F32),
            pltpu.VMEM(qkvw.shape, BF16), pltpu.VMEM(projw.shape, BF16),
            pltpu.VMEM(fc1w.shape, BF16), pltpu.VMEM(fc2w.shape, BF16),
            pltpu.VMEM((padded, 128), jnp.int32),
            pltpu.VMEM((2, 256, width), F32),
            pltpu.VMEM((4, items, 8, width), F32), pltpu.VMEM((items, 8, width), F32),
            pltpu.VMEM((4, 8, width), F32),
            pltpu.VMEM((4, 8, 256), F32), pltpu.VMEM((3, 2, 8, 128), F32),
            dma((7,)), dma((4,)), dma((2,)),
            dma((3,)), dma((3,)), dma((3,)), dma((3,)),
            *[dma((8,)) for _ in range(6)],
        ],
        compiler_params=pltpu.CompilerParams(
            collective_id=0, has_side_effects=True, vmem_limit_bytes=62 * 2**20),
        name="block",
    )(mod_part, ada_b, tok, cot, stops, lim, qkvw, projw, fc1w, fc2w, qv_b, es_row, proj_b, fc1_b, fc2_b)


def shards(
    tokens, cotangent, stop_scales, labels, class_table, ada_weight, ada_bias, qkv_weight, qv_bias, log_scale,
    proj_weight, proj_bias, fc1_weight, fc1_bias, fc2_weight, fc2_bias,
):
    items, slots, width = tokens.shape
    padded = -(-slots // LN_TILE) * LN_TILE
    classes = class_table.shape[0]
    class_local = jnp.concatenate(
        [lax.dynamic_slice_in_dim(class_table, labels[i], 1, 0) for i in range(items)], axis=0).astype(F32)
    lifted = jax.nn.silu(class_local).astype(BF16)
    part = jnp.dot(lifted, ada_weight, preferred_element_type=F32).reshape(items, 6, width)
    part = jnp.pad(part, ((0, 0), (0, 2), (0, 0)))
    ada_rows = jnp.pad(ada_bias.reshape(1, 6, width), ((0, 0), (0, 2), (0, 0)))
    tok = jnp.pad(tokens, ((0, 0), (0, padded - slots), (0, 0)))
    cot = jnp.pad(cotangent, ((0, 0), (0, padded - slots), (0, 0)))
    heads = log_scale.shape[0]
    es_row = jnp.repeat(jnp.exp(log_scale), qkv_weight.shape[2] // heads)[None, :]
    out, tg, g1, g2, gp, gq, modg, small = run_block(
        part, ada_rows, tok, cot, stop_scales, jnp.transpose(qkv_weight, (1, 0, 2)), proj_weight, fc1_weight, fc2_weight,
        qv_bias, es_row, proj_bias[None, :], fc1_bias.reshape(-1, 1, 256), fc2_bias[None, :], slots)

    tag = jnp.broadcast_to(labels.astype(F32)[:, None], (items, width))
    every = lax.all_gather(modg.at[:, 6].set(tag), "dp", axis=0, tiled=True)
    every_label = every[:, 6, 0]
    class_hot = every_label[:, None] == jnp.arange(classes, dtype=F32)[None, :]
    dmod = every[:, :6].reshape(-1, 6 * width)
    dmod = jnp.where(every_label[:, None] >= 0, dmod, 0.0).astype(BF16)
    every_class = jnp.dot(class_hot.astype(BF16), class_table, preferred_element_type=F32)
    every_lift = jax.nn.silu(every_class).astype(BF16)
    lifted_grad = jnp.einsum("ik,dk->id", dmod, ada_weight, preferred_element_type=F32)
    class_grad = jax.vjp(jax.nn.silu, every_class)[1](lifted_grad)[0]
    table_grad = jnp.einsum("ic,id->cd", class_hot.astype(F32), class_grad, precision=lax.Precision.HIGHEST)
    ada_weight_grad = jnp.einsum("id,ik->dk", every_lift, dmod, preferred_element_type=F32)
    ada_bias_grad = jnp.sum(dmod.astype(F32), axis=0)
    g1, g2, gp, gq, small = lax.psum((g1, g2, gp, gq, small), "dp")
    lanes = small[3]
    return (
        out[:, :slots], tg[:, :slots], table_grad, ada_weight_grad, ada_bias_grad,
        jnp.transpose(gq, (1, 0, 2)), lanes[:512].reshape(2, 256), lanes[512:768].reshape(heads, -1).sum(axis=1),
        gp, small[2], g1, small[1], g2, small[0],
    )


def solution(mesh):
    return jax.shard_map(
        shards,
        mesh=mesh,
        in_specs=(
            P("dp", None, None), P("dp", None, None), P("dp"), P("dp"), P(None, "mp"), P("mp", None), P(),
            P(None, None, "mp"), P(None, "mp"), P("mp"), P("mp", None), P(), P(None, "mp"), P("mp"), P("mp", None), P(),
        ),
        out_specs=(
            P("dp", None, None), P("dp", None, None), P(None, "mp"), P("mp", None), P(), P(None, None, "mp"), P(None, "mp"),
            P("mp"), P("mp", None), P(), P(None, "mp"), P("mp"), P("mp", None), P(),
        ),
        check_vma=False,
    )
```

time: 1330 us -> 754 us (0.57); the launches traced: 1310 us -> 753 us
  waiting for transfers between devices: 876 us -> 318 us
  Pallas kernels: 0 us -> 306 us
  local copies, waits for them, and re-layouts: 145 us -> 28.9 us
  matrix products: 103 us -> 8.92 us
  other arithmetic: 91.4 us -> 0.76 us
    psum x4 -> x1, waiting for transfers between devices: 876 us -> 318 us  [shards(): g1, g2, gp, gq, small = lax.psum((g1, g2, gp, gq, small), 'dp')]
    pallas_call x0 -> x1, Pallas kernels: none -> 306 us  [run_block(): pl.pallas_call(functools.partial(block_kernel, slots), out_shape=(jax.Sha...]
    dot_general x31 -> x5, matrix products: 103 us -> 8.92 us  [the longest x1 3.73 us: shards(): jnp.einsum('id,ik->dk', every_lift, dmod, preferred_element_type=F32)]
    reduce_sum x19 -> x2, other arithmetic: 69.7 us -> 0.75 us  [the longest x1 0.63 us: shards(): lanes[512:768].reshape(heads, -1).sum(axis=1)]
    dynamic_update_slice x8 -> x0, local copies, waits for them, and re-layouts: 67.2 us -> none  [shards(): lax.map(attend_back, (query_low, key_low, value_low, mixed_grad, log_tota...]
    unnamed x1 -> x0, blocking collectives: 40.4 us -> none
    psum x1, blocking collectives: 13.2 us -> 39.7 us  [shards(): g1, g2, gp, gq, small = lax.psum((g1, g2, gp, gq, small), 'dp')]
    unnamed x170 -> x27, local copies, waits for them, and re-layouts: 30.3 us -> 11.7 us
  transfers between devices with their start and end apart: 4 -> 1, of which waited for: 4 -> 1; matrix products, arithmetic and copies ran while one was open for 3% -> 2% of each run, Pallas kernels for 0% -> 0%
where the time goes in v1:
time: 754 us; the launch traced here: 753 us
  waiting for transfers between devices  318 us (42%)
  Pallas kernels  306 us (41%)
  blocking collectives  73.7 us (10%)
  local copies, waits for them, and re-layouts  28.9 us (4%)
  between operations  18 us (2%)
  matrix products  8.92 us (1%)
    psum x1, waiting for transfers between devices, shards(): g1, g2, gp, gq, small = lax.psum((g1, g2, gp, gq, small), 'dp')  318 us
    pallas_call x1, Pallas kernels, run_block(): pl.pallas_call(functools.partial(block_kernel, slots), out_shape=(jax.Sha...  306 us
    psum x1, blocking collectives, shards(): g1, g2, gp, gq, small = lax.psum((g1, g2, gp, gq, small), 'dp')  39.7 us
    all_gather x1, blocking collectives, shards(): every = lax.all_gather(modg.at[:, 6].set(tag), 'dp', axis=0, tiled=True)  34 us
  transfers between devices with their start and end apart: 1, of which 1 were waited for; matrix products, arithmetic and copies ran while one was open for 2% of the time, Pallas kernels for 0%

profile of v1, /device:TPU:0, one launch (start us, length us, event | category | flops | bytes accessed | tf_op | source)
XLA Modules:
  0.0 753.4 jit_solution(17365149099020326682)
XLA Ops:
  7.2 0.0 copy-start.3
  7.2 0.0 all-reduce.7.cloned.1.call-start
  7.2 1.4 fusion.27
  11.2 0.7 exp.14
  11.9 0.1 broadcast_in_dim.30
  12.0 0.6 broadcast_in_dim_reshape.3.es_row
  12.6 0.7 reshape.93
  14.7 0.7 constant_dynamic-slice_fusion.1
  15.4 2.4 fusion.15
  17.8 0.0 copy-start.4
  17.9 0.6 pad.18.ada_b
  18.5 0.6 pad.17.mod_part
  19.1 0.0 copy-done.3
  19.1 1.8 pad.19.tok_hbm
  21.0 0.0 copy-done.4
  21.0 1.8 pad.20.cot_hbm
  22.8 305.5 %block.1 = (bf16[2,704,1024]{2,1,0:T(8,128)(2,1)}, bf16[2,704,1024]{2,1,0:T(8,128)(2,1)}, f32[1024,1024]{1,0:T(8,128)}, f32[1024,1024]{1,0:T(8,128)}, f32[256,10...) custom-call(f32[2,8,1024]{2,1,0:T(8,128)} %pad.17.mod_part, ...), custom_call_target="tpu_custom_call" | custom-call | tf_op jit(solution)/shard_map/block/pallas_call | solution.py:571
  328.3 0.0 copy-start.10
  328.4 0.0 all-reduce.7.cloned.1.call-update
  328.4 0.6 copy-done.10
  329.0 0.0 copy-start.9
  329.0 0.0 copy-start.8
  329.0 0.0 copy-start.5
  329.0 3.8 slice.60
  332.8 0.0 copy-done.9
  332.8 39.7 %psum.36 = f32[8,1024]{1,0:T(8,128)S(1)} all-reduce(f32[8,1024]{1,0:T(8,128)S(1)} %copy-done.9), channel_id=1, replica_groups=mesh['dp'=8,'mp'=4] {'dp'}, use_global_device_ids=true, to_apply=%region_2.3 | all-reduce | flops 8192 | bytes 65536 | tf_op jit(solution)/shard_map/psum | solution.py:643
  372.5 0.1 reshape.97
  372.5 0.6 reduce_sum.22
  373.2 0.6 reshape.96
  373.8 0.1 broadcast.48
  373.9 0.0 copy-done.8
  373.9 0.1 scatter.4
  374.0 34.0 %all_gather.3 = f32[16,8,1024]{2,1,0:T(8,128)S(1)} all-gather(f32[2,8,1024]{2,1,0:T(8,128)S(1)} %scatter.4), channel_id=1, replica_groups=mesh['dp'=8,'mp'=4] {'dp'}, dimensions={0}, use_global_device_ids=true | all-gather | bytes 589824 | tf_op jit(solution)/shard_map/all_gather | solution.py:631
  408.0 0.2 slice_reduce_fusion
  408.2 0.1 convert_reduce_fusion
  408.3 0.6 reduce_sum.21
  409.0 0.0 copy-start.7
  409.0 0.1 copy.31
  409.1 0.0 copy-start
  409.1 0.0 copy-done.5
  409.1 1.8 slice.61
  410.9 0.6 fusion.26
  411.5 0.0 copy-done.7
  411.5 0.2 fusion.1
  411.7 0.4 copy-done
  412.1 0.9 fusion.25
  413.0 1.7 fusion
  414.7 3.7 fusion.9
  418.4 317.5 %all-reduce.7.cloned.1.call-done = (f32[1024,3,256]{2,0,1:T(8,128)}, f32[256,1024]{1,0:T(8,128)}, f32[1024,1024]{1,0:T(8,128)}, f32[1024,1024]{1,0:T(8,128)}) async-done(((f32[1024,3,256]{2,0,1:T(8,128)}, f32[256,1024]{1,0:T(8,128)}, f32[1024,1024]{1,0:T(8,128)}, f32[1024,1024]{1,0:T(8,128)}), (f32[1024,3,256]{2,0,1:T(8,128)}, f32[256,1024]{1,0:T(8,128)}, f32[1024,1024]{1,0:T(8,128)}, ...) | async-done | bytes 12582928 | tf_op jit(solution)/shard_map/psum | solution.py:643
  735.9 0.0 copy-start.6
  735.9 0.0 copy-start.2
  735.9 3.9 copy.41
  739.9 0.0 copy-done.6
  739.9 1.0 copy.42
  740.8 0.0 copy-done.2
  740.8 0.0 copy-start.1
  740.8 2.1 copy.43
  743.0 1.6 copy-done.1
  744.5 2.0 copy.44
  (6 shorter events, 0.1 us)
Async XLA Ops:
  7.2 11.9 %copy-start.3 = (bf16[2,680,1024]{2,1,0:T(8,128)(2,1)S(1)}, bf16[2,680,1024]{2,1,0:T(8,128)(2,1)}, u32[]{:S(2)}) copy-start(bf16[2,680,1024]{2,1,0:T(8,128)(2,1)} %param.19) | copy-start | bytes 8355844
  7.2 728.7 %all-reduce.7.cloned.1.call-start = ((), (), s32[]{:S(2)}) async-start(), calls=%async_computation | async-start | bytes 25165824 | tf_op jit(solution)/shard_map/psum | solution.py:643
  17.8 3.1 copy-start.4
  328.3 0.7 copy-start.10
  329.0 3.8 copy-start.9
  329.0 44.9 %copy-start.8 = (f32[2,8,1024]{2,1,0:T(8,128)S(1)}, f32[2,8,1024]{2,1,0:T(8,128)}, u32[]{:S(2)}) copy-start(f32[2,8,1024]{2,1,0:T(8,128)} %get-tuple-element.36) | copy-start | bytes 196612
  329.0 80.1 %copy-start.5 = (bf16[2,704,1024]{2,1,0:T(8,128)(2,1)S(1)}, bf16[2,704,1024]{2,1,0:T(8,128)(2,1)}, u32[]{:S(2)}) copy-start(bf16[2,704,1024]{2,1,0:T(8,128)(2,1)} %get-tuple-element.35) | copy-start | bytes 8650756
  409.0 2.6 copy-start.7
  409.1 3.0 copy-start
  735.9 3.9 copy-start.6
  735.9 4.9 copy-start.2
  740.8 3.7 copy-start.1
Sparse Core Ops, SparseCore 0:
  328.5 407.3 all-reduce.6

commit v2 on v1

v2 whole, which is shorter than its diff:
```python
import functools

import jax
import jax.numpy as jnp
import numpy as np
from jax import lax
from jax.experimental import pallas as pl
from jax.experimental.pallas import tpu as pltpu
from jax.sharding import PartitionSpec as P

SIDE_LIST = (1, 2, 3, 4, 5, 6, 8, 10, 13, 16)
EPSILON = 1e-06
MESH = pl.DeviceIdType.MESH
F32, BF16 = jnp.float32, jnp.bfloat16
GELU_C = 0.7978845608028654
GELU_A = 0.044715
LN_TILE = 64
NT = (((1,), (1,)), ((), ()))
TN = (((0,), (0,)), ((), ()))
NN = (((1,), (0,)), ((), ()))
ATT, DS, DF, BR = 0, 2, 4, 6
X_CHUNKS = (0, 1, 2, 3, 8, 9)


def dot(a, b, dims=NN):
    return lax.dot_general(a, b, dims, preferred_element_type=F32)


def norm_rows(v):
    center = v - jnp.mean(v, axis=-1, keepdims=True)
    scale = lax.rsqrt(jnp.mean(center * center, axis=-1, keepdims=True) + EPSILON)
    return center * scale, scale


def fold(v):
    return jnp.sum(v.reshape(v.shape[0] // 8, 8, v.shape[1]), axis=0)


def head_sum(v, blocks):
    high = v.astype(BF16)
    rest = (v - high.astype(F32)).astype(BF16)
    return dot(high, blocks) + dot(rest, blocks)


def block_kernel(
    slots, n_dp,
    mod_part, ada_b, tok_hbm, cot_hbm, stops, labels, lim_hbm,
    qkvw_hbm, projw_hbm, fc1w_hbm, fc2w_hbm,
    qv_b, es_row, proj_b, fc1_b, fc2_b,
    out_hbm, tg_hbm, final, every, grads, x_in, z_in, mid_in, rest_in,
    tok, cot, fst, sec, dbr, hid, dup,
    att, dst, dfr,
    qk, qkn, mix, dmx, kv, acc,
    rs_buf, y_buf,
    qkvw, projw, fc1w, fc2w, lim,
    stage, modr, mod, g2r, fb1, lanes, sm,
    in_sem, out_sem, load_sem, store_sem,
    mod_s, mod_r, g2_s, g2_r, rs_s, rs_r, y_s, y_r, ag_s, ag_r,
    x1_s, x1_r, zi_s, zi_r, mi_s, mi_r, zo_s, zo_r, x2_s, x2_r, re_s, re_r, ev_s, ev_r,
):
    items, padded, width = tok.shape
    half = width // 2
    me = lax.axis_index("mp")
    dp = lax.axis_index("dp")
    xb = lax.rem(dp, 2)
    z = lax.rem(dp // 2, 4)
    zh = z // 2
    inner = jnp.logical_or(z == 1, z == 2)
    edge = jnp.logical_or(z == 0, z == 3)
    x_mate = dp + 1 - 2 * xb
    z_mate = dp + 2 - 4 * lax.rem(z, 2)
    mid_mate = jnp.where(z == 1, dp + 2, jnp.where(z == 2, dp - 2, dp))
    n_rest = rest_in.shape[0] if n_dp > 8 else 0
    rest_mates = [dp + (8 << k) * (1 - 2 * lax.rem(dp // (8 << k), 2)) for k in range(n_rest)]
    core = lax.rem(me, 2)
    core_mate = me + 1 - 2 * core
    y_mate = lax.rem(me + 2, 4)
    n_ln = padded // LN_TILE
    mt = padded // 2

    def rows_of(t, n):
        return pl.ds(pl.multiple_of(t * n, n), n)

    loads = {}
    for k, (name, src, to) in enumerate((
        ("tok", tok_hbm, tok), ("qkvw", qkvw_hbm, qkvw), ("lim", lim_hbm, lim),
        ("projw", projw_hbm, projw), ("cot", cot_hbm, cot),
        ("fc1w", fc1w_hbm, fc1w), ("fc2w", fc2w_hbm, fc2w),
    )):
        loads[name] = pltpu.make_async_copy(src, to, in_sem.at[k])
        loads[name].start()

    barrier = pltpu.get_barrier_semaphore()
    for step in (1, 2, 3):
        pl.semaphore_signal(barrier, inc=1, device_id={"mp": lax.rem(me + step, 4)}, device_id_type=MESH)
    def greet(step, _):
        pl.semaphore_signal(barrier, inc=1, device_id={"dp": lax.rem(dp + step, n_dp)}, device_id_type=MESH)
        return 0
    lax.fori_loop(1, n_dp, greet, 0)
    pl.semaphore_wait(barrier, 3 + n_dp - 1)

    def share(buf, send, recv):
        copies = []
        for step in (1, 2, 3):
            copies.append(pltpu.make_async_remote_copy(
                src_ref=buf.at[me], dst_ref=buf.at[me], send_sem=send.at[step - 1], recv_sem=recv.at[step - 1],
                device_id={"mp": lax.rem(me + step, 4)}, device_id_type=MESH))
        for copy in copies:
            copy.start()
        return copies

    modr[me] = mod_part[...]
    sent = share(modr, mod_s, mod_r)
    for copy in sent:
        copy.wait()
    mod[...] = ((modr[0] + modr[1]) + (modr[2] + modr[3])) + ada_b[...]

    def vec(i, k):
        return mod[i, k:k + 1, :]

    def rs_copy(buf, i, k):
        return pltpu.make_async_remote_copy(
            src_ref=buf.at[i, 1 - core, pl.ds(0, slots)], dst_ref=rs_buf.at[i], send_sem=rs_s.at[k + i], recv_sem=rs_r.at[k + i],
            device_id={"mp": core_mate}, device_id_type=MESH)

    def y_copy(buf, i, k):
        if k == DS:
            dst = dfr.at[i, 0, pl.ds(0, slots)]
        elif k == BR:
            dst = qk.at[i, pl.ds(0, slots)]
        else:
            dst = y_buf.at[i]
        return pltpu.make_async_remote_copy(
            src_ref=buf.at[i, core, pl.ds(0, slots)], dst_ref=dst, send_sem=y_s.at[k + i], recv_sem=y_r.at[k + i],
            device_id={"mp": y_mate}, device_id_type=MESH)

    def ag_copy(buf, i, k):
        return pltpu.make_async_remote_copy(
            src_ref=buf.at[i, core, pl.ds(0, slots)], dst_ref=buf.at[i, core, pl.ds(0, slots)],
            send_sem=ag_s.at[k + i], recv_sem=ag_r.at[k + i],
            device_id={"mp": core_mate}, device_id_type=MESH)

    add_rows = slots // 5

    def rs_finish(buf, i, k):
        rs_copy(buf, i, k).wait()

        def add(t, _):
            rows = rows_of(t, add_rows)
            buf[i, core, rows, :] = buf[i, core, rows, :] + rs_buf[i, rows, :]
            return 0
        lax.fori_loop(0, 5, add, 0)

    def y_finish(buf, i, k):
        y_copy(buf, i, k).wait()

        def add(t, _):
            rows = rows_of(t, add_rows)
            if k == DS:
                other = dfr[i, 0, rows, :]
            elif k == BR:
                other = qk[i, rows, :]
            else:
                other = y_buf[i, rows, :]
            buf[i, core, rows, :] = buf[i, core, rows, :] + other
            return 0
        lax.fori_loop(0, 5, add, 0)

    def wide(buf, i, rows):
        return jnp.concatenate([buf[i, 0, rows, :], buf[i, 1, rows, :]], axis=1)

    def put_wide(buf, i, rows, v):
        buf[i, 0, rows, :] = v[:, :half]
        buf[i, 1, rows, :] = v[:, half:]

    def blocks_of(n):
        a = lax.broadcasted_iota(jnp.int32, (n, n), 0) // 64
        b = lax.broadcasted_iota(jnp.int32, (n, n), 1) // 64
        return jnp.where(a == b, 1.0, 0.0).astype(BF16)

    ends = np.cumsum(np.array([s * s for s in SIDE_LIST]))
    tiles = ((0, 240, 1, 256), (240, 176, 1, 512), (416, 96, 3, 768))

    def keep_of(i, rows, keys):
        live = jnp.int32(0)
        for s in range(len(SIDE_LIST)):
            live = jnp.where(stops[i] == s + 1, int(ends[s]), live)
        bound = jnp.minimum(lim[rows, :], live)
        n = bound.shape[0]
        return lax.broadcasted_iota(jnp.int32, (n, keys), 1) < bound[:, 0:1]

    def one_head(h):
        lane = lax.broadcasted_iota(jnp.int32, (1, 128), 1) // 64
        return jnp.where(lane == h, 1.0, 0.0).astype(BF16)

    def fill_kv(i, slab):
        for c in (0, 1):
            for h in (0, 1):
                kv[c, h, 0:padded, :] = qkn[i, 1 + c, slab] * one_head(h)

    def exps(i, slab, rows, keys):
        keep = keep_of(i, rows, keys)
        s = dot(qkn[i, 0, slab, rows, :], kv[0, :, 0:keys, :].reshape(2 * keys, 128), NT)
        parts = []
        for h in (0, 1):
            e = jnp.where(keep, jnp.exp(s[:, h * keys:(h + 1) * keys]), 0.0)
            parts.append(e * (1.0 / jnp.sum(e, axis=-1, keepdims=True)))
        return parts

    def each_tile(body):
        for first_row, n, steps, keys in tiles:
            if steps == 1:
                body(pl.ds(first_row, n), keys)
            else:
                def step(t, _, first_row=first_row, n=n, keys=keys):
                    body(pl.ds(pl.multiple_of(first_row + t * n, 16), n), keys)
                    return 0
                lax.fori_loop(0, steps, step, 0)

    def first_norm(i):
        def body(t, _):
            rows = rows_of(t, LN_TILE)
            n, _r = norm_rows(tok[i, rows, :].astype(F32))
            fst[i, rows, :] = (n * (1.0 + vec(i, 2)) + vec(i, 4)).astype(BF16)
            return 0
        lax.fori_loop(0, n_ln, body, 0)

    def project(i):
        blocks = blocks_of(256)

        def body(t, _):
            rows = rows_of(t, mt)
            f = fst[i, rows, :]
            q = dot(f, qkvw[0]) + qv_b[0:1, :]
            qk[i, rows, 0:256] = q
            u = q * lax.rsqrt(head_sum(q * q, blocks) + EPSILON) * es_row[...]
            qkn[i, 0, 0, rows, :] = u[:, :128].astype(BF16)
            qkn[i, 0, 1, rows, :] = u[:, 128:].astype(BF16)
            k = dot(f, qkvw[1])
            qk[i, rows, 256:512] = k
            u = k * lax.rsqrt(head_sum(k * k, blocks) + EPSILON)
            qkn[i, 1, 0, rows, :] = u[:, :128].astype(BF16)
            qkn[i, 1, 1, rows, :] = u[:, 128:].astype(BF16)
            v = dot(f, qkvw[2]) + qv_b[1:2, :]
            qkn[i, 2, 0, rows, :] = v[:, :128].astype(BF16)
            qkn[i, 2, 1, rows, :] = v[:, 128:].astype(BF16)
            return 0
        lax.fori_loop(0, 2, body, 0)

    def attend(i):
        def slab_body(slab, _):
            fill_kv(i, slab)

            def body(rows, keys):
                p = jnp.concatenate([v.astype(BF16) for v in exps(i, slab, rows, keys)], axis=1)
                o = dot(p, kv[1, :, 0:keys, :].reshape(2 * keys, 128))
                mix[i, slab, rows, :] = o.astype(BF16)
            each_tile(body)
            return 0
        lax.fori_loop(0, 2, slab_body, 0)

    def attend_out(i):
        def body(t, _):
            rows = rows_of(t, mt)
            m = jnp.concatenate([mix[i, 0, rows, :], mix[i, 1, rows, :]], axis=1)
            for h in (0, 1):
                att[i, h, rows, :] = dot(m, projw[:, h * half:(h + 1) * half])
            return 0
        lax.fori_loop(0, 2, body, 0)

    def mlp(i):
        def body(t, total):
            rows = rows_of(t, LN_TILE)
            middle = tok[i, rows, :].astype(F32) + vec(i, 0) * (wide(att, i, rows) + proj_b[...])
            n, _r = norm_rows(middle)
            sec[i, rows, :] = (n * (1.0 + vec(i, 3)) + vec(i, 5)).astype(BF16)
            d = (cot[i, rows, :].astype(F32) * vec(i, 1)).astype(BF16)
            dbr[i, rows, :] = d
            return total + fold(d.astype(F32))
        total = lax.fori_loop(0, n_ln, body, jnp.zeros((8, width), F32))
        sm[2, 0:1, :] = sm[2, 0:1, :] + jnp.sum(total, axis=0, keepdims=True)

        def column(j, _):
            cols = pl.ds(pl.multiple_of(j * 256, 256), 256)

            def body(t, _):
                rows = rows_of(t, mt)
                u = dot(sec[i, rows, :], fc1w[:, cols]) + fc1_b[j]
                dh = dot(dbr[i, rows, :], fc2w[cols, :], NT)
                th = jnp.tanh(GELU_C * (u + GELU_A * u * u * u))
                hid[i, rows, cols] = (0.5 * u * (1.0 + th)).astype(BF16)
                slope = 0.5 * (1.0 + th) + 0.5 * u * (1.0 - th * th) * (GELU_C + (3.0 * GELU_C * GELU_A) * u * u)
                d = (dh * slope).astype(BF16)
                dup[i, j, rows, :] = d
                fb1[j] = fb1[j] + fold(d.astype(F32))
                return 0
            lax.fori_loop(0, 2, body, 0)
            return 0
        lax.fori_loop(0, dup.shape[1], column, 0)

        def back(t, _):
            rows = rows_of(t, mt)
            d = jnp.concatenate([dup[i, j, rows, :] for j in range(dup.shape[1])], axis=1)
            for h in (0, 1):
                dst[i, h, rows, :] = dot(d, fc1w[h * half:(h + 1) * half, :], NT)
            return 0
        lax.fori_loop(0, 2, back, 0)

    def half_of(n, h, buf=None):
        return (grads if buf is None else buf).at[n, pl.ds(pl.multiple_of(h * 128, 128), 128)]

    def to_dp(src, to, send, recv, mate):
        return pltpu.make_async_remote_copy(
            src_ref=src, dst_ref=to, send_sem=send, recv_sem=recv, device_id={"dp": mate}, device_id_type=MESH)

    def own(n):
        return xb if n in X_CHUNKS else zh

    def x1(n):
        h = 1 - xb if n in X_CHUNKS else zh
        return to_dp(half_of(n, h), x_in.at[n], x1_s.at[n], x1_r.at[n], x_mate)

    def zin(n):
        if n in X_CHUNKS:
            return to_dp(half_of(n, xb), z_in.at[n, pl.ds(0, 128)], zi_s.at[n], zi_r.at[n], z_mate)
        return to_dp(grads.at[n], z_in.at[n], zi_s.at[n], zi_r.at[n], z_mate)

    def mid(n):
        h = xb if n in X_CHUNKS else 1 - zh
        return to_dp(half_of(n, h), mid_in.at[n], mi_s.at[n], mi_r.at[n], mid_mate)

    def zout(n):
        view = half_of(n, xb, final) if n in X_CHUNKS else final.at[n]
        return to_dp(view, view, zo_s.at[n], zo_r.at[n], z_mate)

    def x2(n):
        return to_dp(half_of(n, xb, final), half_of(n, xb, final), x2_s.at[n], x2_r.at[n], x_mate)

    def swap(n):
        return to_dp(half_of(n, zh, final), half_of(n, zh, final), x2_s.at[n], x2_r.at[n], mid_mate)

    def add_all(pairs, then):
        def load(k):
            rows = pl.ds((k % 2) * 128, 128)
            return [pltpu.make_async_copy(pairs[k][c], stage.at[c, rows], load_sem.at[c, k % 2]) for c in (0, 1)]

        def store(k):
            return pltpu.make_async_copy(stage.at[0, pl.ds((k % 2) * 128, 128)], pairs[k][2 if len(pairs[k]) == 3 else 0], store_sem.at[k % 2])

        def finish(k):
            store(k).wait()
            then(k)
        for copy in load(0):
            copy.start()
        for k in range(len(pairs)):
            if k >= 1:
                finish(k - 1)
            if k + 1 < len(pairs):
                for copy in load(k + 1):
                    copy.start()
            for copy in load(k):
                copy.wait()

            def add(t, _, k=k):
                rows = pl.ds(pl.multiple_of((k % 2) * 128 + t * 16, 16), 16)
                stage[0, rows, :] = stage[0, rows, :] + stage[1, rows, :]
                return 0
            lax.fori_loop(0, 8, add, 0)
            store(k).start()
        finish(len(pairs) - 1)

    def at_edge(body):
        pl.when(edge)(body)

    def at_inner(body):
        pl.when(inner)(body)

    def mid_sum(n, to, then):
        for k in range(n_rest):
            source = mid_in.at[n] if k == 0 else rest_in.at[k - 1, n]
            add_all([(half_of(n, own(n)), source)], lambda _: None)
            copy = to_dp(half_of(n, own(n)), rest_in.at[k, n], re_s.at[k, n], re_r.at[k, n], rest_mates[k])
            copy.start()
            copy.wait()
        source = rest_in.at[n_rest - 1, n] if n_rest else mid_in.at[n]
        add_all([(half_of(n, own(n)), source, half_of(n, own(n), to))], lambda _: then())

    def launch(n):
        if n in X_CHUNKS:
            x1(n).start()
        else:
            at_edge(lambda: zin(n).start())

    def s2(*ns):
        for n in ns:
            if n in X_CHUNKS:
                x1(n).wait()
                add_all([(half_of(n, xb), x_in.at[n])], lambda _: at_edge(lambda: zin(n).start()))
            else:
                @at_inner
                def _():
                    zin(n).wait_recv()
                    view = lambda h: z_in.at[n, pl.ds(pl.multiple_of(h * 128, 128), 128)]
                    add_all([(half_of(n, 1 - zh), view(1 - zh)), (half_of(n, zh), view(zh))],
                            lambda k: mid(n).start() if k == 0 else None)

    def s3(*ns):
        for n in ns:
            @at_inner
            def _():
                if n in X_CHUNKS:
                    zin(n).wait_recv()
                    add_all([(half_of(n, xb), z_in.at[n, pl.ds(0, 128)])], lambda _: mid(n).start())
                else:
                    mid(n).wait()
                    mid_sum(n, grads, lambda: x1(n).start())

    def s4(*ns):
        for n in ns:
            @at_inner
            def _():
                if n in X_CHUNKS:
                    mid(n).wait()
                    mid_sum(n, final, lambda: (zout(n).start(), x2(n).start()))
                else:
                    x1(n).wait()
                    add_all([(half_of(n, zh), x_in.at[n], half_of(n, zh, final))], lambda _: swap(n).start())

    def s5(*ns):
        for n in ns:
            if n in X_CHUNKS:
                @at_edge
                def _():
                    zin(n).wait_send()
                    zout(n).wait_recv()
                    x2(n).start()
            else:
                @at_inner
                def _():
                    swap(n).wait()
                    zout(n).start()

    def s6(*ns):
        for n in ns:
            if n in X_CHUNKS:
                x2(n).wait()
            else:
                @at_edge
                def _():
                    zin(n).wait_send()
                    zout(n).wait_recv()
            at_inner(lambda: zout(n).wait_send())

    def put(slot, n):
        return pltpu.make_async_copy(stage.at[slot], grads.at[n], store_sem.at[slot])

    def produce(ns, make):
        for k, n in enumerate(ns):
            make(k % 2, n)
            put(k % 2, n).start()
            if k >= 1:
                put((k - 1) % 2, ns[k - 1]).wait()
                launch(ns[k - 1])
        put((len(ns) - 1) % 2, ns[-1]).wait()
        launch(ns[-1])

    def both(ref, *rest):
        return jnp.concatenate([ref[(0, *rest)], ref[(1, *rest)]], axis=0)

    def fc_grads(ns):
        def make(slot, n):
            j = n % 4
            cols = pl.ds(j * 256, 256)
            if n < 4:
                stage[slot] = dot(both(hid, slice(None), cols), both(dbr), TN)
            else:
                d = jnp.concatenate([both(dup, m) for m in range(4)], axis=1)
                stage[slot] = dot(both(sec, slice(None), cols), d, TN)
        produce(ns, make)

    def attention_grads(ns):
        def make(slot, n):
            if n == 8:
                for slab in (0, 1):
                    stage[slot, slab * 128:(slab + 1) * 128, :] = dot(both(mix, slab), both(sec), TN)
            else:
                def piece(j, _):
                    cols = pl.ds(pl.multiple_of(j * 256, 256), 256)
                    stage[slot, :, cols] = dot(both(fst, slice(None), cols), both(dup, n - 9), TN)
                    return 0
                lax.fori_loop(0, 4, piece, 0)
        produce(ns, make)

    def second_back(i):
        zero = jnp.zeros((8, width), F32)

        def body(t, sums):
            rows = rows_of(t, LN_TILE)
            attended = wide(att, i, rows) + proj_b[...]
            n, r = norm_rows(tok[i, rows, :].astype(F32) + vec(i, 0) * attended)
            dy = wide(dst, i, rows)
            dn = dy * (1.0 + vec(i, 3))
            dm = cot[i, rows, :].astype(F32) + r * (
                dn - jnp.mean(dn, axis=-1, keepdims=True) - n * jnp.mean(dn * n, axis=-1, keepdims=True))
            put_wide(dst, i, rows, dm)
            da = (dm * vec(i, 0)).astype(BF16)
            sec[i, rows, :] = da
            return (sums[0] + fold(dm * attended), sums[1] + fold(dy * n), sums[2] + fold(dy), sums[3] + fold(da.astype(F32)))
        sums = lax.fori_loop(0, n_ln, body, (zero, zero, zero, zero))
        for k, s in zip((0, 3, 5), sums[:3]):
            sm[i, k:k + 1, :] = jnp.sum(s, axis=0, keepdims=True)
        sm[2, 2:3, :] = sm[2, 2:3, :] + jnp.sum(sums[3], axis=0, keepdims=True)

        def mixed(t, _):
            rows = rows_of(t, mt)
            d = dot(sec[i, rows, :], projw[...], NT)
            dmx[0, rows, :] = d[:, :128].astype(BF16)
            dmx[1, rows, :] = d[:, 128:].astype(BF16)
            return 0
        lax.fori_loop(0, 2, mixed, 0)

    def attend_back(i, slab):
        blocks = blocks_of(128)
        fill_kv(i, slab)
        acc[...] = jnp.zeros_like(acc)

        def body(rows, keys):
            p = exps(i, slab, rows, keys)
            d = dmx[slab, rows, :]
            q = qkn[i, 0, slab, rows, :]
            ds = []
            dp_both = dot(d, kv[1, :, 0:keys, :].reshape(2 * keys, 128), NT)
            for h in (0, 1):
                dpr = dp_both[:, h * keys:(h + 1) * keys]
                ds.append((p[h] * (dpr - jnp.sum(dpr * p[h], axis=-1, keepdims=True))).astype(BF16))
            acc[0, rows, :] = dot(jnp.concatenate(ds, axis=1), kv[0, :, 0:keys, :].reshape(2 * keys, 128))
            kr = pl.ds(0, keys)
            acc[1, kr, :] += dot(
                jnp.concatenate(ds, axis=0), jnp.concatenate([q * one_head(h) for h in (0, 1)], axis=0), TN)
            acc[2, kr, :] += dot(
                jnp.concatenate([v.astype(BF16) for v in p], axis=0),
                jnp.concatenate([d * one_head(h) for h in (0, 1)], axis=0), TN)
        each_tile(body)
        es = es_row[:, slab * 128:(slab + 1) * 128]

        def close(t, sums):
            rows = rows_of(t, LN_TILE)

            def unit(c, g):
                at = c * 256 + slab * 128
                pre = qk[i, rows, at:at + 128]
                r = lax.rsqrt(head_sum(pre * pre, blocks) + EPSILON)
                u = pre * r
                gu = g * u
                return r * (g - u * head_sum(gu, blocks)), gu
            dq, gu = unit(0, acc[0, rows, :] * es)
            dk, _g = unit(1, acc[1, rows, :])
            dq, dk, dv = dq.astype(BF16), dk.astype(BF16), acc[2, rows, :].astype(BF16)
            to = pl.ds(slab * 128, 128)
            dup[i, 0, rows, to] = dq
            dup[i, 1, rows, to] = dk
            dup[i, 2, rows, to] = dv
            return sums[0] + fold(dq.astype(F32)), sums[1] + fold(dv.astype(F32)), sums[2] + fold(gu)
        zero = jnp.zeros((8, 128), F32)
        sums = lax.fori_loop(0, n_ln, close, (zero, zero, zero))
        for k in range(3):
            lanes[k, slab] = lanes[k, slab] + sums[k]

    def first_grad(i):
        def body(t, _):
            rows = rows_of(t, mt)
            for h in (0, 1):
                total = None
                for c in range(3):
                    o = dot(dup[i, c, rows, :], qkvw[c, h * half:(h + 1) * half, :], NT)
                    total = o if total is None else total + o
                dfr[i, h, rows, :] = total
            return 0
        lax.fori_loop(0, 2, body, 0)

    def first_back(i):
        zero = jnp.zeros((8, width), F32)

        def body(t, sums):
            rows = rows_of(t, LN_TILE)
            n, r = norm_rows(tok[i, rows, :].astype(F32))
            dy = wide(dfr, i, rows)
            dn = dy * (1.0 + vec(i, 2))
            g = wide(dst, i, rows) + r * (
                dn - jnp.mean(dn, axis=-1, keepdims=True) - n * jnp.mean(dn * n, axis=-1, keepdims=True))
            fst[i, rows, :] = g.astype(BF16)
            return sums[0] + fold(dy * n), sums[1] + fold(dy)
        sums = lax.fori_loop(0, n_ln, body, (zero, zero))
        for k, s in zip((2, 4), sums):
            sm[i, k:k + 1, :] = jnp.sum(s, axis=0, keepdims=True)
        pltpu.make_async_copy(fst.at[i], tg_hbm.at[i], out_sem.at[i]).start()

    def branch(i):
        def body(t, _):
            rows = rows_of(t, mt)
            for h in (0, 1):
                dst[i, h, rows, :] = dot(hid[i, rows, :], fc2w[:, h * half:(h + 1) * half])
            return 0
        lax.fori_loop(0, 2, body, 0)

        def sums_of(t, sums):
            rows = rows_of(t, LN_TILE)
            g = cot[i, rows, :].astype(F32)
            return sums[0] + fold(g * wide(dst, i, rows)), sums[1] + fold(g)
        zero = jnp.zeros((8, width), F32)
        sums = lax.fori_loop(0, n_ln, sums_of, (zero, zero))
        g2r[me, i:i + 1, :] = jnp.sum(sums[0], axis=0, keepdims=True)
        sm[i, 1:2, :] = fc2_b[...] * jnp.sum(sums[1], axis=0, keepdims=True)

    def block_end(i):
        def body(t, _):
            rows = rows_of(t, LN_TILE)
            middle = tok[i, rows, :].astype(F32) + vec(i, 0) * (wide(att, i, rows) + proj_b[...])
            cot[i, rows, :] = (middle + vec(i, 1) * (wide(dst, i, rows) + fc2_b[...])).astype(BF16)
            return 0
        lax.fori_loop(0, n_ln, body, 0)
        pltpu.make_async_copy(cot.at[i], out_hbm.at[i], out_sem.at[2 + i]).start()

    def every_copy(to, source):
        return pltpu.make_async_remote_copy(
            src_ref=sm, dst_ref=every.at[source], send_sem=ev_s.at[to], recv_sem=ev_r.at[source],
            device_id={"dp": to}, device_id_type=MESH)

    def every_start():
        pltpu.make_async_copy(sm, every.at[dp], out_sem.at[4]).start()

        def body(step, _):
            every_copy(lax.rem(dp + step, n_dp), dp).start()
            return 0
        lax.fori_loop(1, n_dp, body, 0)

    def every_finish():
        pltpu.make_async_copy(sm, every.at[dp], out_sem.at[4]).wait()

        def body(step, _):
            every_copy(lax.rem(dp + step, n_dp), dp).wait_send()
            source = lax.rem(dp + n_dp - step, n_dp)
            every_copy(source, source).wait_recv()
            return 0
        lax.fori_loop(1, n_dp, body, 0)

    def ag(buf, i, k):
        ag_copy(buf, i, k).start()
        ag_copy(buf, i, k).wait()

    sm[...] = jnp.zeros_like(sm)
    fb1[...] = jnp.zeros_like(fb1)
    lanes[...] = jnp.zeros_like(lanes)
    g2r[...] = jnp.zeros_like(g2r)
    kv[...] = jnp.zeros_like(kv)
    for i in (0, 1):
        sm[i, 6:7, :] = jnp.zeros((1, width), F32) + labels[i].astype(F32)
    loads["tok"].wait()
    for i in (0, 1):
        first_norm(i)
        if i == 0:
            loads["qkvw"].wait()
        project(i)
        if i == 0:
            loads["lim"].wait()
        attend(i)
        if i == 0:
            loads["projw"].wait()
        attend_out(i)
        rs_copy(att, i, ATT).start()
        rs_finish(att, i, ATT)
        y_copy(att, i, ATT).start()
    for name in ("cot", "fc1w", "fc2w"):
        loads[name].wait()

    y_finish(att, 0, ATT)
    ag(att, 0, ATT)
    mlp(0)
    rs_copy(dst, 0, DS).start()
    rs_finish(dst, 0, DS)
    y_copy(dst, 0, DS).start()

    y_finish(att, 1, ATT)
    ag(att, 1, ATT)
    mlp(1)
    rs_copy(dst, 1, DS).start()
    fc_grads((4, 0, 5, 1))
    rs_finish(dst, 1, DS)
    y_copy(dst, 1, DS).start()
    fc_grads((6, 2, 7, 3))

    y_finish(dst, 0, DS)
    ag(dst, 0, DS)
    second_back(0)
    attend_back(0, 0)
    s2(4)
    attend_back(0, 1)
    first_grad(0)
    rs_copy(dfr, 0, DF).start()
    s3(4)
    rs_finish(dfr, 0, DF)
    y_copy(dfr, 0, DF).start()
    s2(5)

    y_finish(dst, 1, DS)
    ag(dst, 1, DS)
    second_back(1)
    s2(0, 1, 2, 3)
    attend_back(1, 0)
    s4(4)
    s3(5)
    attend_back(1, 1)
    first_grad(1)
    rs_copy(dfr, 1, DF).start()
    s2(6)
    rs_finish(dfr, 1, DF)
    y_copy(dfr, 1, DF).start()
    s5(4)
    s4(5)
    attention_grads((10, 11, 8, 9))

    y_finish(dfr, 0, DF)
    ag(dfr, 0, DF)
    first_back(0)
    s3(6)
    s2(7)
    s5(5)
    s4(6)
    branch(0)
    rs_copy(dst, 0, BR).start()
    s3(7)
    rs_finish(dst, 0, BR)
    y_copy(dst, 0, BR).start()
    s3(0)
    s5(6)
    s3(1)

    y_finish(dfr, 1, DF)
    ag(dfr, 1, DF)
    first_back(1)
    branch(1)
    rs_copy(dst, 1, BR).start()
    s4(7, 0)
    rs_finish(dst, 1, BR)
    y_copy(dst, 1, BR).start()

    sent = share(g2r, g2_s, g2_r)
    for copy in sent:
        copy.wait()
    total = (g2r[0] + g2r[1]) + (g2r[2] + g2r[3])
    for i in (0, 1):
        sm[i, 1:2, :] = sm[i, 1:2, :] + total[i:i + 1, :]
    for j in range(4):
        sm[2, 1:2, j * 256:(j + 1) * 256] = jnp.sum(fb1[j], axis=0, keepdims=True)
    for k in range(3):
        for slab in (0, 1):
            at = k * 256 + slab * 128
            sm[2, 3:4, at:at + 128] = jnp.sum(lanes[k, slab], axis=0, keepdims=True)
    every_start()
    s2(8, 9)
    s3(2)
    s4(1)
    s5(7)
    s3(3)
    s4(2)

    y_finish(dst, 0, BR)
    ag(dst, 0, BR)
    block_end(0)
    s4(3)
    s5(0, 1)
    s2(10)
    s6(4, 5)
    s3(10)
    s5(2, 3)
    y_finish(dst, 1, BR)
    ag(dst, 1, BR)
    block_end(1)
    s2(11)
    s4(10)
    s3(11)
    s3(8)
    s5(10)
    s3(9)
    s4(11)
    s4(8)
    s5(11)
    s4(9)
    s5(8, 9)
    every_finish()
    s6(0, 1, 2, 3, 6, 7, 10, 11, 8, 9)
    for i in (0, 1):
        pltpu.make_async_copy(fst.at[i], tg_hbm.at[i], out_sem.at[i]).wait()
        pltpu.make_async_copy(cot.at[i], out_hbm.at[i], out_sem.at[2 + i]).wait()


def run_block(n_dp, mod_part, ada_b, tok, cot, stops, labels, qkvw, projw, fc1w, fc2w, qv_b, es_row, proj_b, fc1_b, fc2_b, slots):
    items, padded, width = tok.shape
    half = width // 2
    hidden = fc1w.shape[1]
    n_chunks = 12
    n_rest = max(1, (n_dp // 8).bit_length() - 1)
    ends = np.cumsum(np.array([s * s for s in SIDE_LIST]))
    level = np.minimum(np.searchsorted(ends, np.arange(padded), side="right"), len(SIDE_LIST) - 1)
    lim = jnp.asarray(np.broadcast_to(ends[level][:, None], (padded, 128)), jnp.int32)
    hbm = pl.BlockSpec(memory_space=pl.ANY)
    vmem = pl.BlockSpec(memory_space=pltpu.VMEM)
    smem = pl.BlockSpec(memory_space=pltpu.SMEM)
    wide_b = (items, padded, width)
    wide_f = (items, 2, padded, half)
    dma = pltpu.SemaphoreType.DMA
    return pl.pallas_call(
        functools.partial(block_kernel, slots, n_dp),
        out_shape=(
            jax.ShapeDtypeStruct(wide_b, BF16), jax.ShapeDtypeStruct(wide_b, BF16),
            jax.ShapeDtypeStruct((n_chunks, 256, width), F32), jax.ShapeDtypeStruct((n_dp, 3, 8, width), F32),
            jax.ShapeDtypeStruct((n_chunks, 256, width), F32),
            jax.ShapeDtypeStruct((n_chunks, 128, width), F32), jax.ShapeDtypeStruct((n_chunks, 256, width), F32),
            jax.ShapeDtypeStruct((n_chunks, 128, width), F32), jax.ShapeDtypeStruct((n_rest, n_chunks, 128, width), F32),
        ),
        in_specs=[vmem, vmem, hbm, hbm, smem, smem, hbm, hbm, hbm, hbm, hbm, vmem, vmem, vmem, vmem, vmem],
        out_specs=(hbm,) * 9,
        scratch_shapes=[
            *[pltpu.VMEM(wide_b, BF16) for _ in range(5)],
            pltpu.VMEM((items, padded, hidden), BF16), pltpu.VMEM((items, hidden // 256, padded, 256), BF16),
            *[pltpu.VMEM(wide_f, F32) for _ in range(3)],
            pltpu.VMEM((items, padded, half), F32),
            pltpu.VMEM((items, 3, 2, padded, 128), BF16),
            pltpu.VMEM((items, 2, padded, 128), BF16),
            pltpu.VMEM((2, padded, 128), BF16),
            pltpu.VMEM((2, 2, 768, 128), BF16),
            pltpu.VMEM((3, 768, 128), F32),
            pltpu.VMEM((items, slots, half), F32),
            pltpu.VMEM((items, slots, half), F32),
            pltpu.VMEM(qkvw.shape, BF16), pltpu.VMEM(projw.shape, BF16),
            pltpu.VMEM(fc1w.shape, BF16), pltpu.VMEM(fc2w.shape, BF16),
            pltpu.VMEM((padded, 128), jnp.int32),
            pltpu.VMEM((2, 256, width), F32),
            pltpu.VMEM((4, items, 8, width), F32), pltpu.VMEM((items, 8, width), F32),
            pltpu.VMEM((4, 8, width), F32),
            pltpu.VMEM((4, 8, 256), F32), pltpu.VMEM((3, 2, 8, 128), F32), pltpu.VMEM((3, 8, width), F32),
            dma((7,)), dma((5,)), dma((2, 2)), dma((2,)),
            dma((3,)), dma((3,)), dma((3,)), dma((3,)),
            *[dma((8,)) for _ in range(6)],
            *[dma((n_chunks,)) for _ in range(10)],
            dma((n_rest, n_chunks)), dma((n_rest, n_chunks)), dma((n_dp,)), dma((n_dp,)),
        ],
        compiler_params=pltpu.CompilerParams(
            collective_id=0, has_side_effects=True, vmem_limit_bytes=62 * 2**20),
        name="block",
    )(mod_part, ada_b, tok, cot, stops, labels, lim, qkvw, projw, fc1w, fc2w, qv_b, es_row, proj_b, fc1_b, fc2_b)


def shards(
    n_dp, tokens, cotangent, stop_scales, labels, class_table, ada_weight, ada_bias, qkv_weight, qv_bias, log_scale,
    proj_weight, proj_bias, fc1_weight, fc1_bias, fc2_weight, fc2_bias,
):
    items, slots, width = tokens.shape
    padded = -(-slots // LN_TILE) * LN_TILE
    classes = class_table.shape[0]
    class_local = jnp.concatenate(
        [lax.dynamic_slice_in_dim(class_table, labels[i], 1, 0) for i in range(items)], axis=0).astype(F32)
    lifted = jax.nn.silu(class_local).astype(BF16)
    part = jnp.dot(lifted, ada_weight, preferred_element_type=F32).reshape(items, 6, width)
    part = jnp.pad(part, ((0, 0), (0, 2), (0, 0)))
    ada_rows = jnp.pad(ada_bias.reshape(1, 6, width), ((0, 0), (0, 2), (0, 0)))
    tok = jnp.pad(tokens, ((0, 0), (0, padded - slots), (0, 0)))
    cot = jnp.pad(cotangent, ((0, 0), (0, padded - slots), (0, 0)))
    heads = log_scale.shape[0]
    es_row = jnp.repeat(jnp.exp(log_scale), qkv_weight.shape[2] // heads)[None, :]
    out, tg, grads, every, *_ = run_block(
        n_dp, part, ada_rows, tok, cot, stop_scales, labels, jnp.transpose(qkv_weight, (1, 0, 2)), proj_weight, fc1_weight, fc2_weight,
        qv_bias, es_row, proj_bias[None, :], fc1_bias.reshape(-1, 1, 256), fc2_bias[None, :], slots)

    small = jnp.sum(every[:, 2], axis=0)
    every = every[:, :2].reshape(-1, 8, width)
    every_label = every[:, 6, 0]
    class_hot = every_label[:, None] == jnp.arange(classes, dtype=F32)[None, :]
    dmod = every[:, :6].reshape(-1, 6 * width)
    dmod = jnp.where(every_label[:, None] >= 0, dmod, 0.0).astype(BF16)
    every_class = jnp.dot(class_hot.astype(BF16), class_table, preferred_element_type=F32)
    every_lift = jax.nn.silu(every_class).astype(BF16)
    lifted_grad = jnp.einsum("ik,dk->id", dmod, ada_weight, preferred_element_type=F32)
    class_grad = jax.vjp(jax.nn.silu, every_class)[1](lifted_grad)[0]
    table_grad = jnp.einsum("ic,id->cd", class_hot.astype(F32), class_grad, precision=lax.Precision.HIGHEST)
    ada_weight_grad = jnp.einsum("id,ik->dk", every_lift, dmod, preferred_element_type=F32)
    ada_bias_grad = jnp.sum(dmod.astype(F32), axis=0)
    g2 = grads[0:4].reshape(-1, width)
    g1 = grads[4:8].reshape(-1, width)
    gp = grads[8]
    gq = jnp.transpose(grads[9:12].reshape(3, 256, 4, 256), (2, 1, 0, 3)).reshape(width, 3, 256)
    lanes = small[3]
    return (
        out[:, :slots], tg[:, :slots], table_grad, ada_weight_grad, ada_bias_grad,
        gq, lanes[:512].reshape(2, 256), lanes[512:768].reshape(heads, -1).sum(axis=1),
        gp, small[2], g1, small[1], g2, small[0],
    )


def solution(mesh):
    return jax.shard_map(
        functools.partial(shards, mesh.shape["dp"]),
        mesh=mesh,
        in_specs=(
            P("dp", None, None), P("dp", None, None), P("dp"), P("dp"), P(None, "mp"), P("mp", None), P(),
            P(None, None, "mp"), P(None, "mp"), P("mp"), P("mp", None), P(), P(None, "mp"), P("mp"), P("mp", None), P(),
        ),
        out_specs=(
            P("dp", None, None), P("dp", None, None), P(None, "mp"), P("mp", None), P(), P(None, None, "mp"), P(None, "mp"),
            P("mp"), P("mp", None), P(), P(None, "mp"), P("mp"), P("mp", None), P(),
        ),
        check_vma=False,
    )
```

time: 754 us -> 544 us (0.72); the launches traced: 753 us -> 534 us
  waiting for transfers between devices: 318 us -> 0 us
  Pallas kernels: 306 us -> 480 us
  blocking collectives: 73.7 us -> 0 us
  between operations: 18 us -> 5.08 us
  local copies, waits for them, and re-layouts: 28.9 us -> 37.4 us
    psum x1 -> x0, waiting for transfers between devices: 318 us -> none  [shards(): g1, g2, gp, gq, small = lax.psum((g1, g2, gp, gq, small), 'dp')]
    pallas_call x1, Pallas kernels: 306 us -> 480 us  [run_block(): pl.pallas_call(functools.partial(block_kernel, slots, n_dp), out_shape=(j...]
    psum x1 -> x0, blocking collectives: 39.7 us -> none  [shards(): g1, g2, gp, gq, small = lax.psum((g1, g2, gp, gq, small), 'dp')]
    all_gather x1 -> x0, blocking collectives: 34 us -> none  [shards(): every = lax.all_gather(modg.at[:, 6].set(tag), 'dp', axis=0, tiled=True)]
    unnamed x27 -> x15, local copies, waits for them, and re-layouts: 11.7 us -> 1.96 us
  transfers between devices with their start and end apart: 1 -> 0, of which waited for: 1 -> 0; matrix products, arithmetic and copies ran while one was open for 2% -> 0% of each run, Pallas kernels for 0% -> 0%
where the time goes in v2:
time: 544 us; the launch traced here: 534 us
  Pallas kernels  480 us (88%)
  local copies, waits for them, and re-layouts  37.4 us (7%)
  matrix products  9.96 us (2%)
    pallas_call x1, Pallas kernels, run_block(): pl.pallas_call(functools.partial(block_kernel, slots, n_dp), out_shape=(j...  480 us

profile of v2, /device:TPU:0, one launch (start us, length us, event | category | flops | bytes accessed | tf_op | source)
XLA Modules:
  0.0 534.0 jit_solution(10318644936127819416)
XLA Ops:
  0.6 0.0 copy-start.2
  0.7 0.8 exp.14
  1.5 1.3 fusion.28
  6.7 0.7 constant_dynamic-slice_fusion.1
  7.4 0.1 broadcast_in_dim.26
  7.4 0.6 broadcast_in_dim_reshape.3.es_row
  8.1 0.7 reshape.80
  8.8 0.6 pad.16.ada_b
  9.5 2.4 fusion.15
  11.9 0.0 copy-start.3
  11.9 0.6 pad.15.mod_part
  12.6 0.0 copy-done.2
  12.6 1.9 pad.17.tok_hbm
  14.4 0.0 copy-done.3
  14.4 1.8 pad.18.cot_hbm
  16.3 479.7 %block.1 = (bf16[2,704,1024]{2,1,0:T(8,128)(2,1)}, bf16[2,704,1024]{2,1,0:T(8,128)(2,1)}, f32[12,256,1024]{2,1,0:T(8,128)}, f32[8,3,8,1024]{3,2,1,0:T(8,128)}, f...) custom-call(f32[2,8,1024]{2,1,0:T(8,128)} %pad.15.mod_part, ...), custom_call_target="tpu_custom_call" | custom-call | tf_op jit(solution)/shard_map/block/pallas_call | solution.py:812
  496.0 0.0 copy-start.6
  496.0 0.0 copy-start.1
  496.0 3.8 slice.58
  499.8 0.0 copy-done.6
  499.9 0.0 copy-start.5
  499.9 0.8 copy-done.5
  500.7 0.2 slice_reduce_fusion.1
  500.9 0.1 reshape.87
  501.0 0.6 reduce_sum.32
  501.6 0.6 fusion.27
  502.2 0.6 reshape.86
  502.8 1.2 fusion.1
  504.1 1.2 convert_reduce_fusion
  505.2 1.8 slice.74
  507.0 0.6 reduce_sum.30
  507.6 1.1 copy.35
  508.7 0.0 copy-done.1
  508.7 0.0 copy-start.4
  508.7 0.9 fusion.25
  509.6 1.7 fusion
  511.3 0.0 copy-start
  511.3 2.5 slice_bitcast_fusion
  513.8 0.0 copy-done.4
  513.8 1.8 slice.59
  515.6 2.9 slice.63
  518.5 0.1 copy-done
  518.5 4.2 fusion.26
  522.8 2.9 reshape.84
  525.7 4.1 copy.34
  529.8 3.7 fusion.9
  (6 shorter events, 0.2 us)
Async XLA Ops:
  0.6 11.9 %copy-start.2 = (bf16[2,680,1024]{2,1,0:T(8,128)(2,1)S(1)}, bf16[2,680,1024]{2,1,0:T(8,128)(2,1)}, u32[]{:S(2)}) copy-start(bf16[2,680,1024]{2,1,0:T(8,128)(2,1)} %param.17) | copy-start | bytes 8355844
  11.9 2.5 copy-start.3
  496.0 3.8 copy-start.6
  496.0 12.7 %copy-start.1 = (bf16[256,6144]{1,0:T(8,128)(2,1)S(1)}, bf16[256,6144]{1,0:T(8,128)(2,1)}, u32[]{:S(2)}) copy-start(bf16[256,6144]{1,0:T(8,128)(2,1)} %param.22) | copy-start | bytes 9437188
  499.9 0.8 copy-start.5
  508.7 5.1 copy-start.4
  511.3 7.2 %copy-start = (f32[12,256,1024]{2,1,0:T(8,128)S(1)}, f32[12,256,1024]{2,1,0:T(8,128)}, u32[]{:S(2)}) copy-start(f32[12,256,1024]{2,1,0:T(8,128)} %get-tuple-element.21) | copy-start | bytes 37748740
